TPU v7x, 32 devices: a whole 2x2x4 slice. The times are simulated.
32 devices in a mesh: ens: 2 (over y), tile: 4 (over z), chan: 2 (over x), sec: 2 (over core).
Axes of the slice: x: 2, y: 2, z: 4, core: 2. Of those that a mesh axis runs over, the one named last changes fastest.
Arguments:
- ocean_state: bfloat16 [256, 128, 4, 128], P(('chan', 'sec'), ('ens', 'tile')), parts along dimension 1, may hold values from -6 to 6
- atmos: bfloat16 [16384, 384], P(('ens', 'tile')), parts along dimension 0, may hold values from -6 to 6
- flux_weight: bfloat16 [384, 256], P(None, ('chan', 'sec')), may hold values from -0.3125 to 0.3125
- conv_weight: bfloat16 [9, 256, 256], P(None, None, ('chan', 'sec')), may hold values from -0.125 to 0.125
- conv_bias: bfloat16 [256], P(('chan', 'sec')), may hold values from -3 to 3
- norm_gain: bfloat16 [256], P(('chan', 'sec')), may hold values from 0.5 to 2
- in_weight: bfloat16 [256, 1024], P(None, ('chan', 'sec')), may hold values from -0.375 to 0.375
- in_bias: bfloat16 [1024], P(('chan', 'sec')), may hold values from -3 to 3
- out_weight: bfloat16 [1024, 256], P(('chan', 'sec')), may hold values from -0.25 to 0.25
- layer_scale: bfloat16 [256], P(('chan', 'sec')), may hold values from 0.5 to 2
- cell_mask: int32 [64, 4, 128], P('tile'), may hold values from 0 to 1, as said below
- neighbours: int32 [64, 8], P('tile'), may hold values from -1 to 63, as said below
- remap: int32 [64, 4, 128], P('tile'), may hold values from 0 to 8191
Outputs:
- ocean_next: bfloat16 [256, 128, 4, 128], P(('chan', 'sec'), ('ens', 'tile')), parts along dimension 1
There are 2 independent parts, one for each index of `ens`. A program takes and returns all parts, laid end to end along the dimension named above; an argument that names none is the same for every part. Nothing has to cross between parts.
Inputs may be any that keep to these rules, and one draw needn't show every extreme that they name: `cell_mask`: land cells and every cell of a land block are 0. `neighbours`: for a slot among those of tile index t, each entry is -1 or a slot among those of tile indices t - 1, t and t + 1, i.e. in [(t - 1) * 16, (t + 2) * 16); entries that name land blocks are -1.
All inputs are finite; a program needn't handle non-finite values.
Results may differ from a plain program's by a relative error of at most 0.01.
Values may be sent and summed in bfloat16 or wider, within the bound.
A program may use at most 64 MiB of HBM per device.

v0:
```python
import jax
import jax.numpy as jnp
from jax import lax
from jax.sharding import PartitionSpec as P

norm_eps = 1e-06


def padded_2(cells, sides, width):
    for axis, dim in sides:
        count = lax.axis_size(axis)
        ends = count - 1
        head = lax.slice_in_dim(cells, 0, width, axis=dim)
        tail = lax.slice_in_dim(cells, cells.shape[dim] - width, cells.shape[dim], axis=dim)
        cells = jnp.concatenate(
            [
                lax.ppermute(tail, axis, [(i, (i + 1) % count) for i in range(ends)]),
                cells,
                lax.ppermute(head, axis, [((i + 1) % count, i) for i in range(ends)]),
            ],
            axis=dim,
        )
    return cells


def strips_of(state):
    return jnp.concatenate(
        [
            state[:, :, 0, :],
            state[:, :, -1, :],
            state[:, :, :, 0],
            state[:, :, :, -1],
            state[:, :, 0, 0:1],
            state[:, :, 0, -1:],
            state[:, :, -1, 0:1],
            state[:, :, -1, -1:],
        ],
        axis=2,
    )


def pad_blocks(state, strips, slot_index, valid):
    channels, slot_count, block_rows, block_cols = state.shape
    width = strips.shape[2]
    picked = jnp.take(strips, slot_index.reshape(-1), axis=1).reshape(
        channels, slot_count, 8, width
    )
    picked = jnp.where(valid[None, :, :, None], picked, jnp.zeros_like(picked))
    offset_base = 2 * block_cols + 2 * block_rows
    west_col = picked[:, :, 0, 2 * block_cols + block_rows : offset_base]
    east_col = picked[:, :, 1, 2 * block_cols : 2 * block_cols + block_rows]
    prev_row = picked[:, :, 2, block_cols : 2 * block_cols]
    next_row = picked[:, :, 3, 0:block_cols]
    top_row = jnp.concatenate(
        [
            picked[:, :, 4, offset_base + 3 : offset_base + 4],
            prev_row,
            picked[:, :, 5, offset_base + 2 : offset_base + 3],
        ],
        axis=2,
    )
    bottom_row = jnp.concatenate(
        [
            picked[:, :, 6, offset_base + 1 : offset_base + 2],
            next_row,
            picked[:, :, 7, offset_base : offset_base + 1],
        ],
        axis=2,
    )
    middle = jnp.concatenate([west_col[:, :, :, None], state, east_col[:, :, :, None]], axis=3)
    return jnp.concatenate([top_row[:, :, None, :], middle, bottom_row[:, :, None, :]], axis=2)


def conv_taps(padded, kernel, block_rows, block_cols):
    total = jnp.zeros((kernel.shape[2], padded.shape[1], block_rows, block_cols), jnp.float32)
    for tap in range(9):
        tap_row = tap // 3
        tap_col = tap % 3
        window = padded[:, :, tap_row : tap_row + block_rows, tap_col : tap_col + block_cols]
        total = total + jnp.einsum(
            "cskl,co->oskl", window, kernel[tap], preferred_element_type=jnp.float32
        )
    return total


def add_group(total, pair):
    term = jnp.einsum("hsij,hc->csij", pair[0], pair[1], preferred_element_type=jnp.float32).astype(
        jnp.bfloat16
    )
    term = lax.optimization_barrier(term)
    return (total + term.astype(jnp.float32), None)


def on_device(
    ocean_state,
    atmos,
    flux_weight,
    conv_weight,
    conv_bias,
    norm_gain,
    in_weight,
    in_bias,
    out_weight,
    layer_scale,
    cell_mask,
    neighbours,
    remap,
):
    chan_local, slot_count, block_rows, block_cols = ocean_state.shape
    groups = lax.axis_size(("chan", "sec"))
    channels = chan_local * groups
    hid_local = in_weight.shape[1]
    extended = padded_2(strips_of(ocean_state), (("tile", 1),), slot_count)
    first_slot = (lax.axis_index("tile") - 1) * slot_count
    valid = neighbours >= 0
    slot_index = jnp.clip(neighbours - first_slot, 0, 3 * slot_count - 1)
    padded = pad_blocks(ocean_state, extended, slot_index, valid)
    local_flux = jnp.einsum(
        "rf,fc->cr", atmos, flux_weight, preferred_element_type=jnp.float32
    ).astype(jnp.bfloat16)
    targets = remap.reshape(-1)
    piece = lax.all_gather(local_flux, "tile", axis=1, tiled=True)
    inside = (targets >= 0) & (targets < piece.shape[1])
    values = jnp.take(piece, jnp.clip(targets, 0, piece.shape[1] - 1), axis=1)
    forcing = jnp.where(inside[None, :], values, jnp.zeros_like(values))
    full_kernel, full_bias, full_gain, full_in, full_in_bias, full_out = (
        lax.all_gather(conv_weight, ("chan", "sec"), axis=2, tiled=True),
        lax.all_gather(conv_bias, ("chan", "sec"), axis=0, tiled=True),
        lax.all_gather(norm_gain, ("chan", "sec"), axis=0, tiled=True),
        lax.all_gather(in_weight, ("chan", "sec"), axis=1, tiled=True),
        lax.all_gather(in_bias, ("chan", "sec"), axis=0, tiled=True),
        lax.all_gather(out_weight, ("chan", "sec"), axis=0, tiled=True),
    )
    out_groups = full_out.reshape(groups, hid_local, channels)
    grouped = padded.reshape(
        chan_local, groups, slot_count // groups, block_rows + 2, block_cols + 2
    )
    tiles = lax.all_to_all(grouped, ("chan", "sec"), split_axis=1, concat_axis=0, tiled=True)[:, 0]
    conv_out = (
        conv_taps(tiles, full_kernel, block_rows, block_cols)
        + full_bias.astype(jnp.float32)[:, None, None, None]
    )
    squares = jnp.sum(conv_out * conv_out, axis=0)
    normed = (
        conv_out
        * lax.rsqrt(squares / channels + norm_eps)
        * full_gain.astype(jnp.float32)[:, None, None, None]
    ).astype(jnp.bfloat16)
    pre = jnp.einsum("csij,ch->hsij", normed, full_in, preferred_element_type=jnp.float32)
    hidden = jax.nn.gelu(
        pre + full_in_bias.astype(jnp.float32)[:, None, None, None], approximate=False
    ).astype(jnp.bfloat16)
    hid_groups = hidden.reshape((groups, hid_local) + hidden.shape[1:])
    summed, _ = lax.scan(
        add_group, jnp.zeros((channels,) + hidden.shape[1:], jnp.float32), (hid_groups, out_groups)
    )
    update = lax.all_to_all(
        summed[:, None], ("chan", "sec"), split_axis=0, concat_axis=1, tiled=True
    )
    update = update.reshape(chan_local, slot_count, block_rows, block_cols)
    total = (
        ocean_state.astype(jnp.float32)
        + layer_scale.astype(jnp.float32)[:, None, None, None] * update
    )
    total = total + forcing.reshape(chan_local, slot_count, block_rows, block_cols).astype(
        jnp.float32
    )
    return (cell_mask.astype(jnp.float32)[None] * total).astype(jnp.bfloat16)


def solution(mesh):
    placed = (
        P(("chan", "sec"), ("ens", "tile"), None, None),
        P(("ens", "tile"), None),
        P(None, ("chan", "sec")),
        P(None, None, ("chan", "sec")),
        P(("chan", "sec")),
        P(("chan", "sec")),
        P(None, ("chan", "sec")),
        P(("chan", "sec")),
        P(("chan", "sec"), None),
        P(("chan", "sec")),
        P("tile", None, None),
        P("tile", None),
        P("tile", None, None),
    )
    return jax.shard_map(
        on_device,
        mesh=mesh,
        in_specs=placed,
        out_specs=P(("chan", "sec"), ("ens", "tile"), None, None),
        check_vma=False,
    )
```

profile of v0, /device:TPU:0, one launch (start us, length us, event | category | flops | bytes accessed | tf_op | source)
XLA Modules:
  0.0 303.2 jit_solution(8548367868448448992)
XLA Ops:
  6.5 3.6 %fusion.51 = (bf16[64,16,1,128]{3,2,1,0:T(2,128)(2,1)S(1)}, bf16[64,16,1,128]{3,2,1,0:T(2,128)(2,1)}) fusion(bf16[64,16,4,128]{3,2,1,0:T(4,128)(2,1)} %param.15), kind=kLoop, calls=%fused_computation.95 | loop fusion | bytes 1048576 | tf_op jit(solution)/shard_map/slice | solution.py:30
  24.3 7.2 %copy.136 = bf16[64,16,4,1]{2,0,1,3:T(8,128)(2,1)S(1)} copy(bf16[64,16,4,1]{3,2,1,0:T(4,128)(2,1)} %get-tuple-element.80) | data formatting | bytes 16384 | tf_op jit(solution)/shard_map/squeeze | solution.py:31
  31.6 7.9 %copy.137 = bf16[64,16,4,1]{2,0,1,3:T(8,128)(2,1)} copy(bf16[64,16,4,1]{3,2,1,0:T(4,128)(2,1)} %get-tuple-element.79) | data formatting | bytes 16384 | tf_op jit(solution)/shard_map/squeeze | solution.py:32
  41.6 3.6 %concatenate.40 = bf16[64,16,268]{2,0,1:T(8,128)(2,1)} concatenate(bf16[64,16,128]{2,0,1:T(8,128)(2,1)} %get-tuple-element.89, bf16[64,16,128]{2,0,1:T(8,128)(2,1)} %get-tuple-element.88, bf16[64,16,4]{2,0,1:T(8,128)(2,1)S(1)} %bitcast.225, bf16[64,16,4]{2,0,1:T(8,128)(2,1)} %bitcast.226, bf16[64,16,1]{2,0,1:T(8,128)(2,1)} %copy.73, bf16[64,16,1]{2,0,1:T(8,128)(2,1)} %copy.74, ...), dimensions={2} | concatenate | bytes 1097728 | tf_op jit(solution)/shard_map/concatenate | solution.py:27
  45.3 5.8 %collective-permute-start = (bf16[64,16,268]{2,0,1:T(8,128)(2,1)}, bf16[64,16,268]{2,0,1:T(8,128)(2,1)}, u32[]{:S(2)}, u32[]{:S(2)}) collective-permute-start(bf16[64,16,268]{2,0,1:T(8,128)(2,1)} %concatenate.40), channel_id=1, source_target_pairs={{0,4},{4,8},{8,12},{1,5},{5,9},{9,13},{2,6},{6,10},{10,14},{3,7},{... | collective-permute-start | bytes 1646600 | tf_op jit(solution)/shard_map/ppermute | solution.py:17
  54.4 12.9 %collective-permute-done = bf16[64,16,268]{2,0,1:T(8,128)(2,1)} collective-permute-done((bf16[64,16,268]{2,0,1:T(8,128)(2,1)}, bf16[64,16,268]{2,0,1:T(8,128)(2,1)}, u32[]{:S(2)}, u32[]{:S(2)}) %collective-permute-start) | collective-permute-done | bytes 548896 | tf_op jit(solution)/shard_map/ppermute | solution.py:17
  67.3 5.0 %collective-permute-done.1 = bf16[64,16,268]{2,0,1:T(8,128)(2,1)} collective-permute-done((bf16[64,16,268]{2,0,1:T(8,128)(2,1)}, bf16[64,16,268]{2,0,1:T(8,128)(2,1)}, u32[]{:S(2)}, u32[]{:S(2)}) %collective-permute-start.1) | collective-permute-done | bytes 548896 | tf_op jit(solution)/shard_map/ppermute | solution.py:19
  75.8 5.8 %gather_fusion = bf16[128,64,268]{2,1,0:T(8,128)(2,1)} fusion(bf16[64,48,268]{2,0,1:T(8,128)(2,1)} %pad_maximum_fusion.1, s32[1024]{0:T(1024)S(1)} %pad_clamp_fusion), kind=kCustom, calls=%fused_computation | custom fusion | bytes 8782336 | tf_op jit(solution)/shard_map/jit(_take)/gather | solution.py:45
  81.5 13.8 %copy.78 = bf16[64,16,8,268]{0,1,3,2:T(8,128)(2,1)} copy(bf16[64,16,8,268]{3,0,2,1:T(8,128)(2,1)} %bitcast.217) | data formatting | bytes 8781824 | tf_op jit(solution)/shard_map/jit(_take)/gather | solution.py:45
  95.3 7.9 %select_select_fusion = bf16[64,16,8,268]{0,1,3,2:T(8,128)(2,1)} fusion(bf16[64,16,8,268]{0,1,3,2:T(8,128)(2,1)} %copy.78, pred[16,8]{0,1:T(8,128)(4,1)S(1)} %get-tuple-element.65, pred[16,8]{0,1:T(8,128)(4,1)S(1)} %get-tuple-element.85), kind=kLoop, calls=%fused_computation.10 | loop fusion | flops 4390912 | bytes 8782080 | tf_op jit(solution)/shard_map/jit(_where)/select_n | solution.py:48
  120.3 4.8 %all-to-all-start = ((bf16[64,4,4,6,130]{4,0,3,2,1:T(8,128)(2,1)}), bf16[64,4,4,6,130]{4,0,3,2,1:T(8,128)(2,1)}, u32[]{:S(2)}, u32[]{:S(2)}) async-start(bf16[64,4,4,6,130]{4,0,3,2,1:T(8,128)(2,1)} %pad_maximum_fusion), calls=%async_computation | async-start | bytes 6291456 | tf_op jit(solution)/shard_map/all_to_all | solution.py:138
  128.3 35.2 %all-reduce.2 = (bf16[256]{0:T(256)(128)(2,1)S(1)}, bf16[256]{0:T(256)(128)(2,1)S(1)}) all-reduce(bf16[256]{0:T(256)(128)(2,1)S(1)} %dynamic-update-slice, bf16[256]{0:T(256)(128)(2,1)S(1)} %dynamic-update-slice.1), channel_id=1, replica_groups=mesh['ens'=2,'tile'=4,'chan'=2,'sec'=2] {'chan','sec'}, use_global_device_ids=true, to_apply=%add | all-reduce | flops 512 | bytes 2048
  163.5 5.1 %all-gather = bf16[4,1,256]{2,1,0:T(2,128)(2,1)S(1)} all-gather(bf16[1,1,256]{2,1,0:T(2,128)(2,1)S(1)} %reshape.159), channel_id=1, replica_groups=mesh['ens'=2,'tile'=4,'chan'=2,'sec'=2] {'chan','sec'}, dimensions={0}, use_global_device_ids=true | all-gather | bytes 2560 | tf_op jit(solution)/shard_map/all_gather | solution.py:131
  168.6 7.3 %all_gather.25 = bf16[256,1024]{1,0:T(8,128)(2,1)S(1)} all-gather(bf16[256,256]{1,0:T(8,128)(2,1)S(1)} %copy-done.10), channel_id=1, replica_groups=mesh['ens'=2,'tile'=4,'chan'=2,'sec'=2] {'chan','sec'}, dimensions={1}, use_global_device_ids=true | all-gather | bytes 655360 | tf_op jit(solution)/shard_map/all_gather | solution.py:130
  176.0 7.9 %all_gather.21 = bf16[1024,256]{1,0:T(8,128)(2,1)} all-gather(bf16[256,256]{1,0:T(8,128)(2,1)S(1)} %copy-done.11), channel_id=1, replica_groups=mesh['ens'=2,'tile'=4,'chan'=2,'sec'=2] {'chan','sec'}, dimensions={0}, use_global_device_ids=true | all-gather | bytes 655360 | tf_op jit(solution)/shard_map/all_gather | solution.py:132
  184.0 7.3 %copy.90 = bf16[4,64,1,4,6,130]{1,0,5,4,3,2:T(4,128)(2,1)} copy(bf16[4,64,1,4,6,130]{5,1,4,3,0,2:T(8,128)(2,1)} %bitcast.24) | data formatting | bytes 3194880 | tf_op jit(solution)/shard_map/all_to_all | solution.py:138
  191.3 5.1 %squeeze.76 = bf16[256,4,6,130]{0,3,2,1:T(8,128)(2,1)} reshape(bf16[4,64,1,4,6,130]{1,0,5,4,3,2:T(4,128)(2,1)} %copy.90) | data formatting | bytes 3194880 | tf_op jit(solution)/shard_map/squeeze | solution.py:138
  203.1 20.7 %fusion.7 = bf16[1024,4,4,128]{0,3,2,1:T(8,128)(2,1)} fusion(f32[1024]{0:T(1024)S(1)} %bitcast.239, f32[4,4,128,256]{3,2,1,0:T(8,128)S(1)} %get-tuple-element.87, f32[256]{0:T(256)S(1)} %convert_element_type.43, f32[4,4,128]{2,1,0:T(4,128)S(1)} %add_rsqrt_fusion, bf16[256,1024]{1,0:T(8,128)(2,1)S(1)} %all_gather.25), kind=kOutput, calls=%fused_computation.13 | convolution fusion | flops 1213726720 | bytes 6829056 | tf_op jit(solution)/shard_map/csij,ch->hsij/dot_general | solution.py:149
  223.9 7.9 %reshape.135 = bf16[4,256,4,4,128]{1,0,4,3,2:T(4,128)(2,1)} reshape(bf16[1024,4,4,128]{0,3,2,1:T(8,128)(2,1)} %fusion.7) | data formatting | bytes 8388608 | tf_op jit(solution)/shard_map/reshape | solution.py:153
  231.8 7.5 %copy.101 = bf16[4,256,4,4,128]{4,1,3,2,0:T(8,128)(2,1)} copy(bf16[4,256,4,4,128]{1,0,4,3,2:T(4,128)(2,1)} %reshape.135) | data formatting | bytes 8388608
  239.3 9.9 %while.11 = (s32[]{:T(128)}, f32[256,4,4,128]{3,0,2,1:T(8,128)S(1)}, bf16[4,256,256]{2,1,0:T(8,128)(2,1)}, bf16[4,256,4,4,128]{4,1,3,2,0:T(8,128)(2,1)}, s32[]{:T(128)}, /*index=5*/s32[]{:T(128)}) while((s32[]{:T(128)}, f32[256,4,4,128]{3,0,2,1:T(8,128)S(1)}, bf16[4,256,256]{2,1,0:T(8,128)(2,1)}, ...), condition=%wide.region_2.3_spmd.clone, body=%wide.region_1.2_spmd.clone.sunk | while | flops 270532608 | bytes 7472207 | solution.py:154
  251.8 4.7 %all-to-all-start.1 = ((f32[256,1,4,4,128]{4,3,2,1,0:T(4,128)}), f32[256,1,4,4,128]{4,3,2,1,0:T(4,128)}, u32[]{:S(2)}, u32[]{:S(2)}) async-start(f32[256,1,4,4,128]{4,3,2,1,0:T(4,128)} %bitcast.218), calls=%async_computation.1 | async-start | bytes 4194304 | tf_op jit(solution)/shard_map/all_to_all | solution.py:157
  258.7 29.2 %gather_fusion.1 = bf16[8192,64]{1,0:T(8,128)(2,1)} fusion(bf16[64,8192]{0,1:T(8,128)(2,1)S(1)} %copy.104, s32[8192]{0:T(1024)S(1)} %broadcast_clamp_fusion), kind=kCustom, calls=%fused_computation.1 | custom fusion | bytes 2129920 | tf_op jit(solution)/shard_map/jit(_take)/gather | solution.py:124
  287.9 3.7 %copy.105 = bf16[64,16,4,128]{3,2,1,0:T(4,128)(2,1)} copy(bf16[64,16,4,128]{0,3,2,1:T(8,128)(2,1)} %bitcast.220) | data formatting | bytes 2097152 | tf_op jit(solution)/shard_map/jit(_take)/gather | solution.py:124
  (122 shorter events, 68.7 us)
Async XLA Ops:
  6.5 118.6 %copy-start = (bf16[2048,384]{1,0:T(8,128)(2,1)S(1)}, bf16[2048,384]{1,0:T(8,128)(2,1)}, u32[]{:S(2)}) copy-start(bf16[2048,384]{1,0:T(8,128)(2,1)} %param.16) | copy-start | bytes 4718596
  6.5 3.6 %copy-start.3 = (bf16[64,16,4,128]{3,2,1,0:T(4,128)(2,1)S(1)}, bf16[64,16,4,128]{3,2,1,0:T(4,128)(2,1)}, u32[]{:S(2)}) copy-start(bf16[64,16,4,128]{3,2,1,0:T(4,128)(2,1)} %param.15) | copy-start | bytes 3145732
  6.5 189.8 %all-gather.4.cloned.1.call-start = ((), (), s32[]{:S(2)}) async-start(), calls=%async_computation.2 | async-start | bytes 1474560 | tf_op jit(solution)/shard_map/all_gather | solution.py:127
  39.5 14.8 %copy-start.15 = (s32[16,8]{0,1:T(8,128)S(1)}, s32[16,8]{0,1:T(8,128)}, u32[]{:S(2)}) copy-start(s32[16,8]{0,1:T(8,128)} %param.26) | copy-start | bytes 1540
  45.3 22.0 %collective-permute-start = (bf16[64,16,268]{2,0,1:T(8,128)(2,1)}, bf16[64,16,268]{2,0,1:T(8,128)(2,1)}, u32[]{:S(2)}, u32[]{:S(2)}) collective-permute-start(bf16[64,16,268]{2,0,1:T(8,128)(2,1)} %concatenate.40), channel_id=1, source_target_pairs={{0,4},{4,8},{8,12},{1,5},{5,9},{9,13},{2,6},{6,10},{10,14},{3,7},{... | collective-permute-start | bytes 1646600 | tf_op jit(solution)/shard_map/ppermute | solution.py:17
  51.1 21.2 %collective-permute-start.1 = (bf16[64,16,268]{2,0,1:T(8,128)(2,1)}, bf16[64,16,268]{2,0,1:T(8,128)(2,1)}, u32[]{:S(2)}, u32[]{:S(2)}) collective-permute-start(bf16[64,16,268]{2,0,1:T(8,128)(2,1)} %concatenate.40), channel_id=1, source_target_pairs={{4,0},{8,4},{12,8},{5,1},{9,5},{13,9},{6,2},{10,6},{14,10},{7,3},{... | collective-permute-start | bytes 1646600 | tf_op jit(solution)/shard_map/ppermute | solution.py:19
  107.6 9.6 %copy-start.5 = (bf16[64,16,4,128]{3,0,2,1:T(8,128)(2,1)S(1)}, bf16[64,16,4,128]{3,0,2,1:T(8,128)(2,1)}, u32[]{:S(2)}) copy-start(bf16[64,16,4,128]{3,0,2,1:T(8,128)(2,1)} %copy.82) | copy-start | bytes 3145732
  114.2 2.9 copy-start.6
  114.2 2.9 copy-start.7
  120.2 4.9 %copy-start.13 = (bf16[384,64]{0,1:T(8,128)(2,1)S(1)}, bf16[384,64]{0,1:T(8,128)(2,1)}, u32[]{:S(2)}) copy-start(bf16[384,64]{0,1:T(8,128)(2,1)} %param.17) | copy-start | bytes 147460
  120.2 6.3 %copy-start.20 = (u32[32]{0:T(128)S(1)}, u32[32]{0:T(128)}, u32[]{:S(2)}) copy-start(u32[32]{0:T(128)} %constant.127) | copy-start | bytes 388
  120.2 7.6 %copy-start.16 = (bf16[64]{0:T(256)(128)(2,1)S(1)}, bf16[64]{0:T(256)(128)(2,1)}, u32[]{:S(2)}) copy-start(bf16[64]{0:T(256)(128)(2,1)} %param.19) | copy-start | bytes 388
  120.2 7.8 %copy-start.17 = (bf16[64]{0:T(256)(128)(2,1)S(1)}, bf16[64]{0:T(256)(128)(2,1)}, u32[]{:S(2)}) copy-start(bf16[64]{0:T(256)(128)(2,1)} %param.20) | copy-start | bytes 388
  120.2 43.3 %copy-start.18 = (bf16[256]{0:T(256)(128)(2,1)S(1)}, bf16[256]{0:T(256)(128)(2,1)}, u32[]{:S(2)}) copy-start(bf16[256]{0:T(256)(128)(2,1)} %param.22) | copy-start | bytes 1540
  120.2 48.4 %copy-start.14 = (s32[16,4,128]{2,1,0:T(4,128)S(1)}, s32[16,4,128]{2,1,0:T(4,128)}, u32[]{:S(2)}) copy-start(s32[16,4,128]{2,1,0:T(4,128)} %param.25) | copy-start | bytes 98308
  120.2 48.4 %copy-start.19 = (bf16[64]{0:T(256)(128)(2,1)S(1)}, bf16[64]{0:T(256)(128)(2,1)}, u32[]{:S(2)}) copy-start(bf16[64]{0:T(256)(128)(2,1)} %param.24) | copy-start | bytes 388
  120.3 48.4 %copy-start.10 = (bf16[256,256]{1,0:T(8,128)(2,1)S(1)}, bf16[256,256]{1,0:T(8,128)(2,1)}, u32[]{:S(2)}) copy-start(bf16[256,256]{1,0:T(8,128)(2,1)} %param.21) | copy-start | bytes 393220
  120.3 55.7 %copy-start.11 = (bf16[256,256]{1,0:T(8,128)(2,1)S(1)}, bf16[256,256]{1,0:T(8,128)(2,1)}, u32[]{:S(2)}) copy-start(bf16[256,256]{1,0:T(8,128)(2,1)} %param.23) | copy-start | bytes 393220
  120.3 63.7 %all-to-all-start = ((bf16[64,4,4,6,130]{4,0,3,2,1:T(8,128)(2,1)}), bf16[64,4,4,6,130]{4,0,3,2,1:T(8,128)(2,1)}, u32[]{:S(2)}, u32[]{:S(2)}) async-start(bf16[64,4,4,6,130]{4,0,3,2,1:T(8,128)(2,1)} %pad_maximum_fusion), calls=%async_computation | async-start | bytes 6291456 | tf_op jit(solution)/shard_map/all_to_all | solution.py:138
  125.1 58.9 %copy-start.12 = (s32[16,4,128]{2,1,0:T(4,128)S(1)}, s32[16,4,128]{2,1,0:T(4,128)}, u32[]{:S(2)}) copy-start(s32[16,4,128]{2,1,0:T(4,128)} %param.27) | copy-start | bytes 98308
  125.1 131.5 %all-gather.6.cloned.1.call-start = ((), (), s32[]{:S(2)}) async-start(), calls=%async_computation.3 | async-start | bytes 1310720 | tf_op jit(solution)/shard_map/all_gather | solution.py:122
  251.8 39.8 %all-to-all-start.1 = ((f32[256,1,4,4,128]{4,3,2,1,0:T(4,128)}), f32[256,1,4,4,128]{4,3,2,1,0:T(4,128)}, u32[]{:S(2)}, u32[]{:S(2)}) async-start(f32[256,1,4,4,128]{4,3,2,1,0:T(4,128)} %bitcast.218), calls=%async_computation.1 | async-start | bytes 4194304 | tf_op jit(solution)/shard_map/all_to_all | solution.py:157
  287.9 6.1 %copy-start.4 = (bf16[64,16,4,128]{3,2,1,0:T(4,128)(2,1)S(1)}, bf16[64,16,4,128]{3,2,1,0:T(4,128)(2,1)}, u32[]{:S(2)}) copy-start(bf16[64,16,4,128]{3,2,1,0:T(4,128)(2,1)} %param.15) | copy-start | bytes 3145732
  291.6 4.7 %copy-start.1 = (bf16[2048,384]{1,0:T(8,128)(2,1)S(1)}, bf16[2048,384]{1,0:T(8,128)(2,1)}, u32[]{:S(2)}) copy-start(bf16[2048,384]{1,0:T(8,128)(2,1)} %param.16) | copy-start | bytes 4718596
  (3 other events, 6.3 us)
Sparse Core Ops, SparseCore 0:
  52.7 19.5 all-gather.3
  127.5 27.7 all-gather.5
where the time goes:
time: 305 us; the launch traced here: 303 us
  local copies, waits for them, and re-layouts  140 us (46%)
  blocking collectives  55.6 us (18%)
  matrix products  35.6 us (12%)
  other arithmetic  22.6 us (7%)
  waiting for transfers between devices  17.9 us (6%)
  starting transfers between devices  16.8 us (6%)
  between operations  14.4 us (5%)
    unnamed x1, blocking collectives  35.2 us
    gather x2, local copies, waits for them, and re-layouts, on_device(): values = jnp.take(piece, jnp.clip(targets, 0, piece.shape[1] - 1), axis=1)  33 us
    dot_general x1, matrix products, on_device(): jnp.einsum('csij,ch->hsij', normed, full_in, preferred_element_type=jnp.f...  20.7 us
    gather x2, local copies, waits for them, and re-layouts, pad_blocks(): jnp.take(strips, slot_index.reshape(-1), axis=1)  19.6 us
    unnamed x54, local copies, waits for them, and re-layouts  15.9 us
    ppermute x1, waiting for transfers between devices, padded_2(): lax.ppermute(tail, axis, [(i, (i + 1) % count) for i in range(ends)])  12.9 us
    all_gather x1, blocking collectives, on_device(): lax.all_gather(out_weight, ('chan', 'sec'), axis=0, tiled=True)  7.95 us
    select_n x1, other arithmetic, pad_blocks(): picked = jnp.where(valid[None, :, :, None], picked, jnp.zeros_like(picked))  7.94 us
  transfers between devices with their start and end apart: 6, of which 2 were waited for; matrix products, arithmetic and copies ran while one was open for 51% of the time, Pallas kernels for 0%

commit v1 on v0

v1 whole, which is shorter than its diff:
```python
import functools

import jax
import jax.numpy as jnp
from jax import lax
from jax.experimental import pallas as pl
from jax.experimental.pallas import tpu as pltpu
from jax.sharding import PartitionSpec as P

norm_eps = 1e-06
F32, BF16 = jnp.float32, jnp.bfloat16
LIMIT = 48 * 1024 * 1024


def params():
    return pltpu.CompilerParams(vmem_limit_bytes=LIMIT)


def nt(a, b):
    return lax.dot_general(a, b, (((1,), (1,)), ((), ())), preferred_element_type=F32)


def whole(*shape):
    return pl.BlockSpec(shape, lambda *_: (0,) * len(shape))


def eye(n, m, off=0):
    r = lax.broadcasted_iota(jnp.int32, (n, m), 0)
    c = lax.broadcasted_iota(jnp.int32, (n, m), 1)
    return jnp.where(c == r + off, 1.0, 0.0).astype(BF16)


def pack_weights(cw, vec, iw, ow, out):
    taps, chan, cl = cw.shape
    hl = iw.shape[1]
    for t in range(taps):
        out[t * cl : (t + 1) * cl, :] = cw[t].astype(F32).T.astype(BF16)
    base = taps * cl
    out[base : base + hl, :] = iw[...].astype(F32).T.astype(BF16)
    out[base + hl : base + 2 * hl, :] = ow[...]
    out[base + 2 * hl :, :] = vec[...]


def flux_rows(atm, fw, out):
    cl = fw.shape[1]
    rows = out.shape[0]
    w = fw[...]
    parts = []
    for k in range(atm.shape[0] // rows):
        parts.append(jnp.dot(atm[k * rows : (k + 1) * rows, :], w, preferred_element_type=F32))
    out[...] = jnp.concatenate(parts, axis=1).astype(BF16)


def split_rows(state, rows_out, strips, scr):
    s = pl.program_id(0)
    slots = pl.num_programs(0)
    cl, _, bh, bw = state.shape
    scr[...] = state[:, 0].astype(F32)

    @pl.when(s == 0)
    def _():
        strips[slots] = jnp.zeros(strips.shape[1:], BF16)

    lane = lax.broadcasted_iota(jnp.int32, (cl, bw), 1)
    edge = strips[slots, :, 0:bw].astype(F32)
    for i in range(bh):
        row = scr[:, i, :]
        edge = jnp.where(lane == s * 8 + i, row[:, 0:1], edge)
        edge = jnp.where(lane == s * 8 + 4 + i, row[:, bw - 1 : bw], edge)
        cells = row.astype(BF16)
        rows_out[0, :, i * bw : (i + 1) * bw] = cells
        if i == 0:
            strips[s, :, 0:bw] = cells
        if i == bh - 1:
            strips[s, :, bw : 2 * bw] = cells
    strips[slots, :, 0:bw] = edge.astype(BF16)


def halo(near, rows, below, mine, above, out, ext):
    s = pl.program_id(0)
    slots = pl.num_programs(0)
    cl = rows.shape[1]
    bw = 128
    width = rows.shape[2]

    @pl.when(s == 0)
    def _():
        ext[0] = below[...]
        ext[1] = mine[...]
        ext[2] = above[...]

    lane = lax.broadcasted_iota(jnp.int32, (cl, bw), 1)

    def place(k):
        n = near[s, k]
        ok = n >= 0
        m = jnp.maximum(n, 0)
        return ok, m // slots, lax.rem(m, slots)

    def strip(k, lo):
        ok, t, m = place(k)
        got = ext[t, m, :, lo : lo + bw].astype(F32)
        return jnp.where(ok, got, 0.0).astype(BF16)

    out[0, :, 0:bw] = strip(2, bw)
    out[0, :, bw : bw + width] = rows[0]
    out[0, :, bw + width : 2 * bw + width] = strip(3, 0)
    edge = jnp.zeros((cl, bw), F32)
    for k, src, dst, count in (
        (4, 7, 0, 1), (0, 4, 1, 4), (6, 4, 5, 1), (5, 3, 6, 1), (1, 0, 7, 4), (7, 0, 11, 1),
    ):
        ok, t, m = place(k)
        turned = pltpu.roll(
            ext[t, slots, :, 0:bw].astype(F32), lax.rem(dst - src - m * 8 + 2 * bw, bw), 1
        )
        here = (lane >= dst) & (lane < dst + count)
        edge = jnp.where(here, jnp.where(ok, turned, 0.0), edge)
    out[0, :, 2 * bw + width :] = edge.astype(BF16)


def block(tile, pack, out, xs, hid, *, hl):
    groups, _, cl, width = tile.shape
    chan = groups * cl
    bw = 128
    rows = width // bw - 1
    cells = (rows - 2) * bw
    x = tile[:, 0].reshape(chan, width)
    edge = x[:, rows * bw :].astype(F32)
    lane = lax.broadcasted_iota(jnp.int32, (chan, bw), 1)
    for i in range(rows):
        mid = x[:, i * bw : (i + 1) * bw]
        wide = mid.astype(F32)
        left = jnp.where(lane == 0, edge[:, i : i + 1], pltpu.roll(wide, 1, 1))
        right = jnp.where(lane == bw - 1, edge[:, rows + i : rows + i + 1], pltpu.roll(wide, bw - 1, 1))
        at = slice(i * bw, (i + 1) * bw)
        xs[0:chan, at] = left.astype(BF16)
        xs[chan : 2 * chan, at] = mid
        xs[2 * chan : 3 * chan, at] = right.astype(BF16)
    base = 9 * cl
    ident = eye(256, 256)
    cols = [nt(ident, pack[g, base + 2 * hl :, :]) for g in range(groups)]
    bias = jnp.concatenate([c[:cl, 1:2] for c in cols], axis=0)
    gain = jnp.concatenate([c[:cl, 2:3] for c in cols], axis=0)
    acc = jnp.zeros((chan, cells), F32)
    for a in range(3):
        for b in range(3):
            t = 3 * a + b
            w = pack[:, t * cl : (t + 1) * cl, :].reshape(chan, chan)
            acc += jnp.dot(
                w, xs[b * chan : (b + 1) * chan, a * bw : a * bw + cells], preferred_element_type=F32
            )
    acc = acc + bias
    squares = jnp.sum(acc * acc, axis=0, keepdims=True)
    normed = (acc * lax.rsqrt(squares / chan + norm_eps) * gain).astype(BF16)
    for g in range(groups):
        pre = jnp.dot(pack[g, base : base + hl, :], normed, preferred_element_type=F32)
        pre = pre + cols[g][:hl, 0:1]
        act = 0.5 * pre * (1.0 + lax.erf(pre * 0.7071067811865476))
        hid[g * hl : (g + 1) * hl, :] = act.astype(BF16)
    ow = pack[:, base + hl : base + 2 * hl, :].reshape(groups * hl, chan)
    upd = lax.dot_general(ow, hid[...], (((0,), (0,)), ((), ())), preferred_element_type=F32)
    out[:, 0] = upd.astype(BF16).reshape(groups, cl, cells)


def pick(index, table, which, out, wide, got, *, cl):
    s = pl.program_id(0)
    cells = got.shape[0]
    parts = 128 // cl

    @pl.when(s == 0)
    def _():
        wide[...] = table[...].astype(F32)

    def body(j, c):
        for u in range(16):
            at = j * 16 + u
            got[pl.ds(at, 1), :] = wide[pl.ds(index[s * cells + at], 1), :]
        return c

    lax.fori_loop(0, cells // 16, body, 0)
    rows = got[...].astype(BF16)
    part = which[0]
    total = jnp.zeros((cl, cells), F32)
    for k in range(parts):
        total = jnp.where(part == k, nt(eye(cl, 128, k * cl), rows), total)
    out[0] = total.astype(BF16)


def finish(rows, update, force, mask, scale, out, scr):
    cl, _, bh, bw = out.shape
    total = rows[0].astype(F32) + scale[:, 0:1].astype(F32) * update[0].astype(F32)
    total = (total + force[0].astype(F32)) * mask[0].astype(F32)
    for i in range(bh):
        scr[:, i, :] = total[:, i * bw : (i + 1) * bw]
    out[:, 0] = scr[...].astype(BF16)


def on_device(
    ocean_state, atmos, flux_weight, conv_weight, conv_bias, norm_gain, in_weight, in_bias,
    out_weight, layer_scale, cell_mask, neighbours, remap,
):
    cl, slots, bh, bw = ocean_state.shape
    groups = lax.axis_size(("chan", "sec"))
    tiles = lax.axis_size("tile")
    chan = groups * cl
    hl = in_weight.shape[1]
    cells = bh * bw
    per = slots // groups
    width = cells + 3 * bw

    state_spec = pl.BlockSpec((cl, 1, bh, bw), lambda s, *_: (0, s, 0, 0))
    slot_spec = pl.BlockSpec((1, cl, cells), lambda s, *_: (s, 0, 0))
    rows, strips = pl.pallas_call(
        split_rows,
        grid=(slots,),
        in_specs=[state_spec],
        out_specs=[slot_spec, whole(slots + 1, cl, 2 * bw)],
        out_shape=[
            jax.ShapeDtypeStruct((slots, cl, cells), BF16),
            jax.ShapeDtypeStruct((slots + 1, cl, 2 * bw), BF16),
        ],
        scratch_shapes=[pltpu.VMEM((cl, bh, bw), F32)],
        compiler_params=params(),
        name="split_rows",
    )(ocean_state)
    below = lax.ppermute(strips, "tile", [(i, i + 1) for i in range(tiles - 1)])
    above = lax.ppermute(strips, "tile", [(i + 1, i) for i in range(tiles - 1)])

    vec = jnp.stack(
        [jnp.pad(v, (0, chan - v.shape[0])) for v in (in_bias, conv_bias, norm_gain)]
    )
    vec = jnp.pad(vec, ((0, 13), (0, 0)))
    pack_rows = 9 * cl + 2 * hl + 16
    pack = pl.pallas_call(
        pack_weights,
        out_shape=jax.ShapeDtypeStruct((pack_rows, chan), BF16),
        compiler_params=params(),
        name="pack_weights",
    )(conv_weight, vec, in_weight, out_weight)
    pack = lax.all_gather(pack, ("chan", "sec"), axis=0)

    parts = 128 // cl
    trows = atmos.shape[0] // parts
    table = pl.pallas_call(
        flux_rows,
        out_shape=jax.ShapeDtypeStruct((trows, 128), BF16),
        compiler_params=params(),
        name="flux_rows",
    )(atmos, flux_weight)
    table = lax.all_gather(table, "tile", axis=0, tiled=True)

    local = lax.rem(remap, trows * parts)
    flat = (remap // (trows * parts)) * trows + lax.rem(local, trows)
    which = (local // trows).reshape(slots, 1, cells)
    lane_spec = pl.BlockSpec((1, 1, cells), lambda s, *_: (s, 0, 0))
    forcing = pl.pallas_call(
        functools.partial(pick, cl=cl),
        grid_spec=pltpu.PrefetchScalarGridSpec(
            num_scalar_prefetch=1,
            grid=(slots,),
            in_specs=[whole(tiles * trows, 128), lane_spec],
            out_specs=slot_spec,
            scratch_shapes=[pltpu.VMEM((tiles * trows, 128), F32), pltpu.VMEM((cells, 128), F32)],
        ),
        out_shape=jax.ShapeDtypeStruct((slots, cl, cells), BF16),
        compiler_params=params(),
        cost_estimate=pl.CostEstimate(flops=10**10, bytes_accessed=4 * 10**6, transcendentals=0),
        name="pick",
    )(flat.reshape(-1), table, which)

    first = (lax.axis_index("tile") - 1) * slots
    near = jnp.where(neighbours >= 0, jnp.clip(neighbours - first, 0, 3 * slots - 1), -1)
    strip_spec = whole(slots + 1, cl, 2 * bw)
    padded = pl.pallas_call(
        halo,
        grid_spec=pltpu.PrefetchScalarGridSpec(
            num_scalar_prefetch=1,
            grid=(slots,),
            in_specs=[slot_spec, strip_spec, strip_spec, strip_spec],
            out_specs=pl.BlockSpec((1, cl, width), lambda s, *_: (s, 0, 0)),
            scratch_shapes=[pltpu.VMEM((3, slots + 1, cl, 2 * bw), BF16)],
        ),
        out_shape=jax.ShapeDtypeStruct((slots, cl, width), BF16),
        compiler_params=params(),
        name="halo",
    )(near, rows, below, strips, above)
    tile = lax.all_to_all(
        padded.reshape(groups, per, cl, width), ("chan", "sec"), split_axis=0, concat_axis=0
    )
    update = pl.pallas_call(
        functools.partial(block, hl=hl),
        grid=(per,),
        in_specs=[
            pl.BlockSpec((groups, 1, cl, width), lambda s: (0, s, 0, 0)),
            whole(groups, pack_rows, chan),
        ],
        out_specs=pl.BlockSpec((groups, 1, cl, cells), lambda s: (0, s, 0, 0)),
        out_shape=jax.ShapeDtypeStruct((groups, per, cl, cells), BF16),
        scratch_shapes=[
            pltpu.VMEM((3 * chan, (bh + 2) * bw), BF16),
            pltpu.VMEM((groups * hl, cells), BF16),
        ],
        compiler_params=params(),
        name="block",
    )(tile, pack)
    update = lax.all_to_all(update, ("chan", "sec"), split_axis=0, concat_axis=0)
    return pl.pallas_call(
        finish,
        grid=(slots,),
        in_specs=[slot_spec, slot_spec, slot_spec, lane_spec, whole(cl, 1)],
        out_specs=state_spec,
        out_shape=jax.ShapeDtypeStruct(ocean_state.shape, BF16),
        scratch_shapes=[pltpu.VMEM((cl, bh, bw), F32)],
        compiler_params=params(),
        name="finish",
    )(
        rows,
        update.reshape(slots, cl, cells),
        forcing,
        cell_mask.reshape(slots, 1, cells),
        layer_scale.reshape(cl, 1),
    )


def solution(mesh):
    placed = (
        P(("chan", "sec"), ("ens", "tile"), None, None),
        P(("ens", "tile"), None),
        P(None, ("chan", "sec")),
        P(None, None, ("chan", "sec")),
        P(("chan", "sec")),
        P(("chan", "sec")),
        P(None, ("chan", "sec")),
        P(("chan", "sec")),
        P(("chan", "sec"), None),
        P(("chan", "sec")),
        P("tile", None, None),
        P("tile", None),
        P("tile", None, None),
    )
    return jax.shard_map(
        on_device,
        mesh=mesh,
        in_specs=placed,
        out_specs=P(("chan", "sec"), ("ens", "tile"), None, None),
        check_vma=False,
    )
```

time: 305 us -> 126 us (0.41)
  local copies, waits for them, and re-layouts: 140 us -> 11.8 us
  blocking collectives: 55.6 us -> 0 us
  Pallas kernels: 0 us -> 49.7 us
  matrix products: 35.6 us -> 0 us
  other arithmetic: 22.6 us -> 0.1 us
  waiting for transfers between devices: 17.9 us -> 35.9 us
    gather x4 -> x0, local copies, waits for them, and re-layouts: 52.5 us -> none  [the longest x2 33 us: on_device(): values = jnp.take(piece, jnp.clip(targets, 0, piece.shape[1] - 1), axis=1)]
    pallas_call x0 -> x7, Pallas kernels: none -> 49.7 us  [the longest x1 15.8 us: on_device(): pl.pallas_call(functools.partial(pick, cl=cl), grid_spec=pltpu.PrefetchSc...]
    dot_general x15 -> x0, matrix products: 35.6 us -> none  [the longest x1 20.7 us: on_device(): jnp.einsum('csij,ch->hsij', normed, full_in, preferred_element_type=jnp.f...]
    unnamed x1 -> x0, blocking collectives: 35.2 us -> none
    squeeze x8 -> x0, local copies, waits for them, and re-layouts: 26 us -> none  [the longest x1 7.9 us: strips_of(): state[:, :, :, -1]]
    all_to_all x2, waiting for transfers between devices: 0.01 us -> 22.6 us  [the longest x1 22.6 us: on_device(): lax.all_to_all(padded.reshape(groups, per, cl, width), ('chan', 'sec'), s...]
    all_gather x3 -> x0, blocking collectives: 20.4 us -> none  [the longest x1 7.95 us: on_device(): lax.all_gather(out_weight, ('chan', 'sec'), axis=0, tiled=True)]
    slice x8 -> x0, local copies, waits for them, and re-layouts: 13.4 us -> none  [the longest x1 3.64 us: strips_of(): state[:, :, -1, :]]
  transfers between devices with their start and end apart: 6 -> 6, of which waited for: 2 -> 3; matrix products, arithmetic and copies ran while one was open for 51% -> 0% of each run, Pallas kernels for 0% -> 33%
where the time goes in v1:
time: 126 us; the launch traced here: 125 us
  Pallas kernels  49.7 us (39%)
  waiting for transfers between devices  35.9 us (28%)
  starting transfers between devices  14.3 us (11%)
  between operations  13.5 us (11%)
  local copies, waits for them, and re-layouts  11.8 us (9%)
    all_to_all x1, waiting for transfers between devices, on_device(): lax.all_to_all(padded.reshape(groups, per, cl, width), ('chan', 'sec'), s...  22.6 us
    pallas_call x1, Pallas kernels, on_device(): pl.pallas_call(functools.partial(pick, cl=cl), grid_spec=pltpu.PrefetchSc...  15.8 us
    unnamed x29, local copies, waits for them, and re-layouts  9.73 us
    pallas_call x1, Pallas kernels, on_device(): pl.pallas_call(functools.partial(block, hl=hl), grid=(per,), in_specs=[pl...  9.18 us
    pallas_call x1, Pallas kernels, on_device(): pl.pallas_call(halo, grid_spec=pltpu.PrefetchScalarGridSpec(num_scalar_pr...  8.19 us
    ppermute x1, waiting for transfers between devices, on_device(): below = lax.ppermute(strips, 'tile', [(i, i + 1) for i in range(tiles - 1)])  8.16 us
    pallas_call x1, Pallas kernels, on_device(): pl.pallas_call(split_rows, grid=(slots,), in_specs=[state_spec], out_spec...  7.26 us
    pallas_call x1, Pallas kernels, on_device(): pl.pallas_call(finish, grid=(slots,), in_specs=[slot_spec, slot_spec, slo...  6.8 us
  transfers between devices with their start and end apart: 6, of which 3 were waited for; matrix products, arithmetic and copies ran while one was open for 0% of the time, Pallas kernels for 33%

profile of v1, /device:TPU:0, one launch (start us, length us, event | category | flops | bytes accessed | tf_op | source)
XLA Modules:
  0.0 125.3 jit_solution(9515602611178571677)
XLA Ops:
  6.5 1.3 %copy.16.cw = bf16[9,256,64]{2,1,0:T(8,128)(2,1)S(1)} copy(bf16[9,256,64]{1,2,0:T(8,128)(2,1)} %param.16) | data formatting | bytes 589824 | tf_op args[3]
  7.8 0.7 pad.11
  8.5 0.7 pad.12
  9.9 0.9 copy-done.5
  10.8 0.9 copy-done.6
  11.7 1.1 pack_weights.1
  12.8 1.3 %copy-done.2 = bf16[64,16,4,128]{3,2,1,0:T(4,128)(2,1)S(1)} copy-done((bf16[64,16,4,128]{3,2,1,0:T(4,128)(2,1)S(1)}, bf16[64,16,4,128]{3,2,1,0:T(4,128)(2,1)}, u32[]{:S(2)}) %copy-start.2) | copy-done | bytes 1048600
  14.2 7.3 %split_rows.1 = (bf16[16,64,512]{2,1,0:T(8,128)(2,1)S(1)}, bf16[17,64,256]{2,1,0:T(8,128)(2,1)S(1)}) custom-call(bf16[64,16,4,128]{3,2,1,0:T(4,128)(2,1)S(1)} %copy-done.2), custom_call_target="tpu_custom_call" | custom-call | tf_op jit(solution)/shard_map/split_rows/pallas_call | solution.py:213
  21.4 5.8 %collective-permute-start = (bf16[17,64,256]{2,1,0:T(8,128)(2,1)S(1)}, bf16[17,64,256]{2,1,0:T(8,128)(2,1)}, u32[]{:S(2)}, u32[]{:S(2)}) collective-permute-start(bf16[17,64,256]{2,1,0:T(8,128)(2,1)S(1)} %get-tuple-element.8.mine), channel_id=1, source_target_pairs={{0,4},{4,8},{8,12},{1,5},{5,9},{9,13},{2,6},{6,10},{10,14},{3,7},{... | collective-permute-start | bytes 1671176 | tf_op jit(solution)/shard_map/ppermute | solution.py:226
  27.2 1.3 %collective-permute-start.1 = (bf16[17,64,256]{2,1,0:T(8,128)(2,1)S(1)}, bf16[17,64,256]{2,1,0:T(8,128)(2,1)}, u32[]{:S(2)}, u32[]{:S(2)}) collective-permute-start(bf16[17,64,256]{2,1,0:T(8,128)(2,1)S(1)} %get-tuple-element.8.mine), channel_id=1, source_target_pairs={{4,0},{8,4},{12,8},{5,1},{9,5},{13,9},{6,2},{10,6},{14,10},{7,3},{... | collective-permute-start | bytes 1671176 | tf_op jit(solution)/shard_map/ppermute | solution.py:227
  28.6 1.3 %flux_rows.1 = bf16[1024,128]{1,0:T(8,128)(2,1)} custom-call(bf16[2048,384]{1,0:T(8,128)(2,1)S(1)} %copy-done.1, bf16[384,64]{1,0:T(8,128)(2,1)S(1)} %copy.17.fw), custom_call_target="tpu_custom_call" | custom-call | tf_op jit(solution)/shard_map/flux_rows/pallas_call | solution.py:244
  30.1 8.2 %collective-permute-done.below = bf16[17,64,256]{2,1,0:T(8,128)(2,1)} collective-permute-done((bf16[17,64,256]{2,1,0:T(8,128)(2,1)S(1)}, bf16[17,64,256]{2,1,0:T(8,128)(2,1)}, u32[]{:S(2)}, u32[]{:S(2)}) %collective-permute-start) | collective-permute-done | bytes 557088 | tf_op jit(solution)/shard_map/ppermute | solution.py:226
  38.2 5.0 %collective-permute-done.1.above = bf16[17,64,256]{2,1,0:T(8,128)(2,1)} collective-permute-done((bf16[17,64,256]{2,1,0:T(8,128)(2,1)S(1)}, bf16[17,64,256]{2,1,0:T(8,128)(2,1)}, u32[]{:S(2)}, u32[]{:S(2)}) %collective-permute-start.1) | collective-permute-done | bytes 557088 | tf_op jit(solution)/shard_map/ppermute | solution.py:227
  43.2 8.2 %halo.1 = bf16[16,64,896]{2,1,0:T(8,128)(2,1)} custom-call(s32[16,8]{1,0:T(8,128)S(1)} %clamp_select_fusion.near, bf16[16,64,512]{2,1,0:T(8,128)(2,1)S(1)} %get-tuple-element.7.rows, bf16[17,64,256]{2,1,0:T(8,128)(2,1)} %collective-permute-done.below, bf16[17,64,256]{2,1,0:T(8,128)(2,1)S(1)} %get-tuple-element.8.mine, ...), custom_call_target="tpu_custom_call" | custom-call | tf_op jit(solution)/shard_map/halo/pallas_call | solution.py:274
  51.4 3.7 %all-to-all-start = ((bf16[4,4,64,896]{3,2,1,0:T(8,128)(2,1)}), bf16[4,4,64,896]{3,2,1,0:T(8,128)(2,1)S(1)}, u32[]{:S(2)}, u32[]{:S(2)}) async-start(bf16[4,4,64,896]{3,2,1,0:T(8,128)(2,1)} %bitcast), calls=%async_computation | async-start | bytes 3670016 | tf_op jit(solution)/shard_map/all_to_all | solution.py:287
  55.4 22.6 %all-to-all-done.tile = bf16[4,4,64,896]{3,2,1,0:T(8,128)(2,1)S(1)} async-done(((bf16[4,4,64,896]{3,2,1,0:T(8,128)(2,1)}), bf16[4,4,64,896]{3,2,1,0:T(8,128)(2,1)S(1)}, u32[]{:S(2)}, u32[]{:S(2)}) %all-to-all-start) | async-done | bytes 1835040 | tf_op jit(solution)/shard_map/all_to_all | solution.py:287
  78.0 1.6 %copy-done = bf16[4416,256]{1,0:T(8,128)(2,1)S(1)} copy-done((bf16[4416,256]{1,0:T(8,128)(2,1)S(1)}, bf16[4416,256]{1,0:T(8,128)(2,1)}, u32[]{:S(2)}) %copy-start) | copy-done | bytes 2261016
  79.7 9.2 %block.1 = bf16[4,4,64,512]{3,2,1,0:T(8,128)(2,1)} custom-call(bf16[4,4,64,896]{3,2,1,0:T(8,128)(2,1)S(1)} %all-to-all-done.tile, bf16[4,1104,256]{2,1,0:T(8,128)(2,1)S(1)} %bitcast.8), custom_call_target="tpu_custom_call" | custom-call | tf_op jit(solution)/shard_map/block/pallas_call | solution.py:290
  88.8 3.5 %all-to-all-start.1 = ((bf16[4,4,64,512]{3,2,1,0:T(8,128)(2,1)}), bf16[4,4,64,512]{3,2,1,0:T(8,128)(2,1)S(1)}, u32[]{:S(2)}, u32[]{:S(2)}) async-start(bf16[4,4,64,512]{3,2,1,0:T(8,128)(2,1)} %block.1), calls=%async_computation.1 | async-start | bytes 2097152 | tf_op jit(solution)/shard_map/all_to_all | solution.py:306
  92.4 1.2 copy-done.8
  93.6 15.8 %pick.1.force = bf16[16,64,512]{2,1,0:T(8,128)(2,1)S(1)} custom-call(s32[8192]{0:T(1024)S(1)} %bitcast.11, bf16[4096,128]{1,0:T(8,128)(2,1)S(1)} %copy-done.8, s32[16,1,512]{2,1,0:T(1,128)S(1)} %bitcast.10), custom_call_target="tpu_custom_call" | custom-call | flops 10000000000 | bytes 4000000 | tf_op jit(solution)/shard_map/pick/pallas_call | solution.py:256
  109.5 1.0 copy-done.3
  110.5 1.2 copy-done.4
  111.7 6.8 %finish.1 = bf16[64,16,4,128]{3,2,1,0:T(4,128)(2,1)} custom-call(bf16[16,64,512]{2,1,0:T(8,128)(2,1)S(1)} %get-tuple-element.7.rows, bf16[16,64,512]{2,1,0:T(8,128)(2,1)S(1)} %bitcast.7, bf16[16,64,512]{2,1,0:T(8,128)(2,1)S(1)} %copy-done.4, s32[16,1,512]{2,1,0:T(1,128)S(1)} %bitcast.9, bf16[64,1]{1,0:T(8,128)(2,1)S(1)} %copy.18.scale), custom_call_target="tpu_custom_call" | custom-call | tf_op jit(solution)/shard_map/finish/pallas_call | solution.py:307
  (35 shorter events, 1.2 us)
Async XLA Ops:
  6.5 21.9 %copy-start.9 = (bf16[384,64]{0,1:T(8,128)(2,1)S(1)}, bf16[384,64]{0,1:T(8,128)(2,1)}, u32[]{:S(2)}) copy-start(bf16[384,64]{0,1:T(8,128)(2,1)} %param.15) | copy-start | bytes 147460
  6.5 71.5 %all-gather.6.cloned.1.call-start = ((), (), s32[]{:S(2)}) async-start(), calls=%async_computation.3 | async-start | bytes 2826240 | tf_op jit(solution)/shard_map/all_gather | solution.py:240
  9.8 0.9 copy-start.5
  10.8 0.9 copy-start.6
  12.7 15.9 %copy-start.1 = (bf16[2048,384]{1,0:T(8,128)(2,1)S(1)}, bf16[2048,384]{1,0:T(8,128)(2,1)}, u32[]{:S(2)}) copy-start(bf16[2048,384]{1,0:T(8,128)(2,1)} %atm.1) | copy-start | bytes 4718596
  12.8 79.6 %all-gather.4.cloned.1.call-start = ((), (), s32[]{:S(2)}) async-start(), calls=%async_computation.2 | async-start | bytes 1310720 | tf_op jit(solution)/shard_map/all_gather | solution.py:250
  12.8 1.3 %copy-start.2 = (bf16[64,16,4,128]{3,2,1,0:T(4,128)(2,1)S(1)}, bf16[64,16,4,128]{3,2,1,0:T(4,128)(2,1)}, u32[]{:S(2)}) copy-start(bf16[64,16,4,128]{3,2,1,0:T(4,128)(2,1)} %state.1) | copy-start | bytes 3145732
  14.2 15.8 %copy-start.11 = (s32[16,8]{0,1:T(8,128)S(1)}, s32[16,8]{0,1:T(8,128)}, u32[]{:S(2)}) copy-start(s32[16,8]{0,1:T(8,128)} %param.24) | copy-start | bytes 1540
  21.4 16.8 %collective-permute-start = (bf16[17,64,256]{2,1,0:T(8,128)(2,1)S(1)}, bf16[17,64,256]{2,1,0:T(8,128)(2,1)}, u32[]{:S(2)}, u32[]{:S(2)}) collective-permute-start(bf16[17,64,256]{2,1,0:T(8,128)(2,1)S(1)} %get-tuple-element.8.mine), channel_id=1, source_target_pairs={{0,4},{4,8},{8,12},{1,5},{5,9},{9,13},{2,6},{6,10},{10,14},{3,7},{... | collective-permute-start | bytes 1671176 | tf_op jit(solution)/shard_map/ppermute | solution.py:226
  27.2 16.1 %collective-permute-start.1 = (bf16[17,64,256]{2,1,0:T(8,128)(2,1)S(1)}, bf16[17,64,256]{2,1,0:T(8,128)(2,1)}, u32[]{:S(2)}, u32[]{:S(2)}) collective-permute-start(bf16[17,64,256]{2,1,0:T(8,128)(2,1)S(1)} %get-tuple-element.8.mine), channel_id=1, source_target_pairs={{4,0},{8,4},{12,8},{5,1},{9,5},{13,9},{6,2},{10,6},{14,10},{7,3},{... | collective-permute-start | bytes 1671176 | tf_op jit(solution)/shard_map/ppermute | solution.py:227
  51.4 3.7 %copy-start.12 = (bf16[64]{0:T(256)(128)(2,1)S(1)}, bf16[64]{0:T(256)(128)(2,1)}, u32[]{:S(2)}) copy-start(bf16[64]{0:T(256)(128)(2,1)} %param.22) | copy-start | bytes 388
  51.4 3.9 %copy-start.10 = (s32[16,4,128]{2,1,0:T(4,128)S(1)}, s32[16,4,128]{2,1,0:T(4,128)}, u32[]{:S(2)}) copy-start(s32[16,4,128]{2,1,0:T(4,128)} %param.25) | copy-start | bytes 98308
  51.4 26.6 %all-to-all-start = ((bf16[4,4,64,896]{3,2,1,0:T(8,128)(2,1)}), bf16[4,4,64,896]{3,2,1,0:T(8,128)(2,1)S(1)}, u32[]{:S(2)}, u32[]{:S(2)}) async-start(bf16[4,4,64,896]{3,2,1,0:T(8,128)(2,1)} %bitcast), calls=%async_computation | async-start | bytes 3670016 | tf_op jit(solution)/shard_map/all_to_all | solution.py:287
  78.0 1.6 %copy-start = (bf16[4416,256]{1,0:T(8,128)(2,1)S(1)}, bf16[4416,256]{1,0:T(8,128)(2,1)}, u32[]{:S(2)}) copy-start(bf16[4416,256]{1,0:T(8,128)(2,1)} %all-gather.6.cloned.1.call-done) | copy-start | bytes 6782980
  88.8 21.6 %all-to-all-start.1 = ((bf16[4,4,64,512]{3,2,1,0:T(8,128)(2,1)}), bf16[4,4,64,512]{3,2,1,0:T(8,128)(2,1)S(1)}, u32[]{:S(2)}, u32[]{:S(2)}) async-start(bf16[4,4,64,512]{3,2,1,0:T(8,128)(2,1)} %block.1), calls=%async_computation.1 | async-start | bytes 2097152 | tf_op jit(solution)/shard_map/all_to_all | solution.py:306
  92.4 1.2 copy-start.8
  93.6 16.9 %copy-start.7 = (s32[16,4,128]{2,1,0:T(4,128)S(1)}, s32[16,4,128]{2,1,0:T(4,128)}, u32[]{:S(2)}) copy-start(s32[16,4,128]{2,1,0:T(4,128)} %param.23) | copy-start | bytes 98308
  109.5 1.0 copy-start.3
  110.5 1.2 copy-start.4
Sparse Core Ops, SparseCore 0:
  12.9 26.1 all-gather.5
  40.7 27.9 all-gather.3

commit v2 on v1

--- a/solution.py
+++ b/solution.py
@@ -53,82 +53,83 @@
 
 def split_rows(state, rows_out, strips, scr):
     s = pl.program_id(0)
-    slots = pl.num_programs(0)
-    cl, _, bh, bw = state.shape
-    scr[...] = state[:, 0].astype(F32)
+    cl, some, bh, bw = state.shape
+    last = strips.shape[0] - 1
 
     @pl.when(s == 0)
     def _():
-        strips[slots] = jnp.zeros(strips.shape[1:], BF16)
+        strips[last] = jnp.zeros(strips.shape[1:], BF16)
 
     lane = lax.broadcasted_iota(jnp.int32, (cl, bw), 1)
-    edge = strips[slots, :, 0:bw].astype(F32)
-    for i in range(bh):
-        row = scr[:, i, :]
-        edge = jnp.where(lane == s * 8 + i, row[:, 0:1], edge)
-        edge = jnp.where(lane == s * 8 + 4 + i, row[:, bw - 1 : bw], edge)
-        cells = row.astype(BF16)
-        rows_out[0, :, i * bw : (i + 1) * bw] = cells
-        if i == 0:
-            strips[s, :, 0:bw] = cells
-        if i == bh - 1:
-            strips[s, :, bw : 2 * bw] = cells
-    strips[slots, :, 0:bw] = edge.astype(BF16)
-
-
-def halo(near, rows, below, mine, above, out, ext):
-    s = pl.program_id(0)
-    slots = pl.num_programs(0)
-    cl = rows.shape[1]
+    edge = strips[last, :, 0:bw].astype(F32)
+    for j in range(some):
+        scr[...] = state[:, j].astype(F32)
+        slot = s * some + j
+        for i in range(bh):
+            row = scr[:, i, :]
+            edge = jnp.where(lane == slot * 8 + i, row[:, 0:1], edge)
+            edge = jnp.where(lane == slot * 8 + 4 + i, row[:, bw - 1 : bw], edge)
+            cells = row.astype(BF16)
+            rows_out[j, :, i * bw : (i + 1) * bw] = cells
+            if i == 0:
+                strips[slot, :, 0:bw] = cells
+            if i == bh - 1:
+                strips[slot, :, bw : 2 * bw] = cells
+    strips[last, :, 0:bw] = edge.astype(BF16)
+
+
+def halo(near, below, mine, above, out, *, per):
+    g = pl.program_id(0)
+    slots = per * pl.num_programs(0)
+    cl = out.shape[2]
     bw = 128
-    width = rows.shape[2]
-
-    @pl.when(s == 0)
-    def _():
-        ext[0] = below[...]
-        ext[1] = mine[...]
-        ext[2] = above[...]
-
     lane = lax.broadcasted_iota(jnp.int32, (cl, bw), 1)
 
-    def place(k):
-        n = near[s, k]
-        ok = n >= 0
-        m = jnp.maximum(n, 0)
-        return ok, m // slots, lax.rem(m, slots)
-
-    def strip(k, lo):
-        ok, t, m = place(k)
-        got = ext[t, m, :, lo : lo + bw].astype(F32)
-        return jnp.where(ok, got, 0.0).astype(BF16)
-
-    out[0, :, 0:bw] = strip(2, bw)
-    out[0, :, bw : bw + width] = rows[0]
-    out[0, :, bw + width : 2 * bw + width] = strip(3, 0)
+    def choose(t, m, at):
+        got = jnp.where(t == 1, mine[m, :, at].astype(F32), below[m, :, at].astype(F32))
+        return jnp.where(t == 2, above[m, :, at].astype(F32), got)
+
     edge = jnp.zeros((cl, bw), F32)
-    for k, src, dst, count in (
-        (4, 7, 0, 1), (0, 4, 1, 4), (6, 4, 5, 1), (5, 3, 6, 1), (1, 0, 7, 4), (7, 0, 11, 1),
-    ):
-        ok, t, m = place(k)
-        turned = pltpu.roll(
-            ext[t, slots, :, 0:bw].astype(F32), lax.rem(dst - src - m * 8 + 2 * bw, bw), 1
-        )
-        here = (lane >= dst) & (lane < dst + count)
-        edge = jnp.where(here, jnp.where(ok, turned, 0.0), edge)
-    out[0, :, 2 * bw + width :] = edge.astype(BF16)
-
-
-def block(tile, pack, out, xs, hid, *, hl):
-    groups, _, cl, width = tile.shape
+    for j in range(per):
+
+        def place(k):
+            n = near[g * per + j, k]
+            m = jnp.maximum(n, 0)
+            return n >= 0, m // slots, lax.rem(m, slots)
+
+        for k, lo, unit in ((2, bw, 0), (3, 0, 1)):
+            ok, t, m = place(k)
+            got = choose(t, m, slice(lo, lo + bw))
+            out[0, 2 * j + unit] = jnp.where(ok, got, 0.0).astype(BF16)
+        for k, src, dst, count in (
+            (4, 7, 0, 1), (0, 4, 1, 4), (6, 4, 5, 1), (5, 3, 6, 1), (1, 0, 7, 4), (7, 0, 11, 1),
+        ):
+            ok, t, m = place(k)
+            to = j * 12 + dst
+            turned = pltpu.roll(
+                choose(t, slots, slice(0, bw)), lax.rem(to - src - m * 8 + 2 * bw, bw), 1
+            )
+            here = (lane >= to) & (lane < to + count)
+            edge = jnp.where(here, jnp.where(ok, turned, 0.0), edge)
+    out[0, 2 * per] = edge.astype(BF16)
+
+
+def block(tile, rim, pack, out, xs, hid, *, hl):
+    groups, _, cl, cells = tile.shape
     chan = groups * cl
     bw = 128
-    rows = width // bw - 1
-    cells = (rows - 2) * bw
-    x = tile[:, 0].reshape(chan, width)
-    edge = x[:, rows * bw :].astype(F32)
+    rows = cells // bw + 2
+    s = pl.program_id(0)
+    edge = rim[:, rim.shape[1] - 1].reshape(chan, bw).astype(F32)
+    edge = pltpu.roll(edge, lax.rem(bw - s * 12, bw), 1)
     lane = lax.broadcasted_iota(jnp.int32, (chan, bw), 1)
     for i in range(rows):
-        mid = x[:, i * bw : (i + 1) * bw]
+        if i == 0:
+            mid = rim[:, 2 * s].reshape(chan, bw)
+        elif i == rows - 1:
+            mid = rim[:, 2 * s + 1].reshape(chan, bw)
+        else:
+            mid = tile[:, 0, :, (i - 1) * bw : i * bw].reshape(chan, bw)
         wide = mid.astype(F32)
         left = jnp.where(lane == 0, edge[:, i : i + 1], pltpu.roll(wide, 1, 1))
         right = jnp.where(lane == bw - 1, edge[:, rows + i : rows + i + 1], pltpu.roll(wide, bw - 1, 1))
@@ -187,12 +188,14 @@
 
 
 def finish(rows, update, force, mask, scale, out, scr):
-    cl, _, bh, bw = out.shape
-    total = rows[0].astype(F32) + scale[:, 0:1].astype(F32) * update[0].astype(F32)
-    total = (total + force[0].astype(F32)) * mask[0].astype(F32)
-    for i in range(bh):
-        scr[:, i, :] = total[:, i * bw : (i + 1) * bw]
-    out[:, 0] = scr[...].astype(BF16)
+    cl, some, bh, bw = out.shape
+    gain = scale[:, 0:1].astype(F32)
+    for j in range(some):
+        total = rows[j].astype(F32) + gain * update[j].astype(F32)
+        total = (total + force[j].astype(F32)) * mask[j].astype(F32)
+        for i in range(bh):
+            scr[:, i, :] = total[:, i * bw : (i + 1) * bw]
+        out[:, j] = scr[...].astype(BF16)
 
 
 def on_device(
@@ -206,15 +209,16 @@
     hl = in_weight.shape[1]
     cells = bh * bw
     per = slots // groups
-    width = cells + 3 * bw
-
-    state_spec = pl.BlockSpec((cl, 1, bh, bw), lambda s, *_: (0, s, 0, 0))
+    some = 4
+
+    state_spec = pl.BlockSpec((cl, some, bh, bw), lambda s, *_: (0, s, 0, 0))
+    some_spec = pl.BlockSpec((some, cl, cells), lambda s, *_: (s, 0, 0))
     slot_spec = pl.BlockSpec((1, cl, cells), lambda s, *_: (s, 0, 0))
     rows, strips = pl.pallas_call(
         split_rows,
-        grid=(slots,),
+        grid=(slots // some,),
         in_specs=[state_spec],
-        out_specs=[slot_spec, whole(slots + 1, cl, 2 * bw)],
+        out_specs=[some_spec, whole(slots + 1, cl, 2 * bw)],
         out_shape=[
             jax.ShapeDtypeStruct((slots, cl, cells), BF16),
             jax.ShapeDtypeStruct((slots + 1, cl, 2 * bw), BF16),
@@ -223,6 +227,9 @@
         compiler_params=params(),
         name="split_rows",
     )(ocean_state)
+    tile = lax.all_to_all(
+        rows.reshape(groups, per, cl, cells), ("chan", "sec"), split_axis=0, concat_axis=0
+    )
     below = lax.ppermute(strips, "tile", [(i, i + 1) for i in range(tiles - 1)])
     above = lax.ppermute(strips, "tile", [(i + 1, i) for i in range(tiles - 1)])
 
@@ -239,6 +246,7 @@
     )(conv_weight, vec, in_weight, out_weight)
     pack = lax.all_gather(pack, ("chan", "sec"), axis=0)
 
+    below, above, atmos = lax.optimization_barrier((below, above, atmos))
     parts = 128 // cl
     trows = atmos.shape[0] // parts
     table = pl.pallas_call(
@@ -271,27 +279,26 @@
     first = (lax.axis_index("tile") - 1) * slots
     near = jnp.where(neighbours >= 0, jnp.clip(neighbours - first, 0, 3 * slots - 1), -1)
     strip_spec = whole(slots + 1, cl, 2 * bw)
-    padded = pl.pallas_call(
-        halo,
+    units = 2 * per + 1
+    rim = pl.pallas_call(
+        functools.partial(halo, per=per),
         grid_spec=pltpu.PrefetchScalarGridSpec(
             num_scalar_prefetch=1,
-            grid=(slots,),
-            in_specs=[slot_spec, strip_spec, strip_spec, strip_spec],
-            out_specs=pl.BlockSpec((1, cl, width), lambda s, *_: (s, 0, 0)),
-            scratch_shapes=[pltpu.VMEM((3, slots + 1, cl, 2 * bw), BF16)],
+            grid=(groups,),
+            in_specs=[strip_spec, strip_spec, strip_spec],
+            out_specs=pl.BlockSpec((1, units, cl, bw), lambda s, *_: (s, 0, 0, 0)),
         ),
-        out_shape=jax.ShapeDtypeStruct((slots, cl, width), BF16),
+        out_shape=jax.ShapeDtypeStruct((groups, units, cl, bw), BF16),
         compiler_params=params(),
         name="halo",
-    )(near, rows, below, strips, above)
-    tile = lax.all_to_all(
-        padded.reshape(groups, per, cl, width), ("chan", "sec"), split_axis=0, concat_axis=0
-    )
+    )(near, below, strips, above)
+    rim = lax.all_to_all(rim, ("chan", "sec"), split_axis=0, concat_axis=0)
     update = pl.pallas_call(
         functools.partial(block, hl=hl),
         grid=(per,),
         in_specs=[
-            pl.BlockSpec((groups, 1, cl, width), lambda s: (0, s, 0, 0)),
+            pl.BlockSpec((groups, 1, cl, cells), lambda s: (0, s, 0, 0)),
+            whole(groups, units, cl, bw),
             whole(groups, pack_rows, chan),
         ],
         out_specs=pl.BlockSpec((groups, 1, cl, cells), lambda s: (0, s, 0, 0)),
@@ -302,12 +309,15 @@
         ],
         compiler_params=params(),
         name="block",
-    )(tile, pack)
+    )(tile, rim, pack)
     update = lax.all_to_all(update, ("chan", "sec"), split_axis=0, concat_axis=0)
     return pl.pallas_call(
         finish,
-        grid=(slots,),
-        in_specs=[slot_spec, slot_spec, slot_spec, lane_spec, whole(cl, 1)],
+        grid=(slots // some,),
+        in_specs=[
+            some_spec, some_spec, some_spec,
+            pl.BlockSpec((some, 1, cells), lambda s: (s, 0, 0)), whole(cl, 1),
+        ],
         out_specs=state_spec,
         out_shape=jax.ShapeDtypeStruct(ocean_state.shape, BF16),
         scratch_shapes=[pltpu.VMEM((cl, bh, bw), F32)],

time: 126 us -> 117 us (0.929)
  Pallas kernels: 49.7 us -> 42.1 us
  starting transfers between devices: 14.3 us -> 16.9 us
  local copies, waits for them, and re-layouts: 11.8 us -> 9.48 us
  waiting for transfers between devices: 35.9 us -> 34.2 us
    pallas_call x3, Pallas kernels: 22.2 us -> 14.6 us  [the longest x1 7.22 us: on_device(): pl.pallas_call(split_rows, grid=(slots // some,), in_specs=[state_spec],...]
    all_to_all x1 -> x2, starting transfers between devices: 3.72 us -> 7 us  [the longest x1 3.53 us: on_device(): lax.all_to_all(rows.reshape(groups, per, cl, cells), ('chan', 'sec'), spl...]
    all_to_all x1 -> x2, waiting for transfers between devices: 22.6 us -> 19.6 us  [the longest x1 10.3 us: on_device(): lax.all_to_all(rows.reshape(groups, per, cl, cells), ('chan', 'sec'), spl...]
    unnamed x29, local copies, waits for them, and re-layouts: 9.73 us -> 7.37 us
    ppermute x1, waiting for transfers between devices: 8.16 us -> 10.4 us  [on_device(): below = lax.ppermute(strips, 'tile', [(i, i + 1) for i in range(tiles - 1)])]
  transfers between devices with their start and end apart: 6 -> 7, of which waited for: 3 -> 4; matrix products, arithmetic and copies ran while one was open for 0% -> 0% of each run, Pallas kernels for 33% -> 31%
where the time goes in v2:
time: 117 us; the launch traced here: 116 us
  Pallas kernels  42.1 us (36%)
  waiting for transfers between devices  34.2 us (29%)
  starting transfers between devices  16.9 us (14%)
  between operations  13.6 us (12%)
  local copies, waits for them, and re-layouts  9.48 us (8%)
    pallas_call x1, Pallas kernels, on_device(): pl.pallas_call(functools.partial(pick, cl=cl), grid_spec=pltpu.PrefetchSc...  15.8 us
    ppermute x1, waiting for transfers between devices, on_device(): below = lax.ppermute(strips, 'tile', [(i, i + 1) for i in range(tiles - 1)])  10.4 us
    all_to_all x1, waiting for transfers between devices, on_device(): lax.all_to_all(rows.reshape(groups, per, cl, cells), ('chan', 'sec'), spl...  10.3 us
    all_to_all x1, waiting for transfers between devices, on_device(): rim = lax.all_to_all(rim, ('chan', 'sec'), split_axis=0, concat_axis=0)  9.3 us
    pallas_call x1, Pallas kernels, on_device(): pl.pallas_call(functools.partial(block, hl=hl), grid=(per,), in_specs=[pl...  9.19 us
    unnamed x29, local copies, waits for them, and re-layouts  7.37 us
    pallas_call x1, Pallas kernels, on_device(): pl.pallas_call(split_rows, grid=(slots // some,), in_specs=[state_spec],...  7.22 us
    ppermute x1, starting transfers between devices, on_device(): below = lax.ppermute(strips, 'tile', [(i, i + 1) for i in range(tiles - 1)])  5.08 us
  transfers between devices with their start and end apart: 7, of which 4 were waited for; matrix products, arithmetic and copies ran while one was open for 0% of the time, Pallas kernels for 31%

profile of v2, /device:TPU:0, one launch (start us, length us, event | category | flops | bytes accessed | tf_op | source)
XLA Modules:
  0.0 116.4 jit_solution(4047272216160828686)
XLA Ops:
  6.5 1.4 %copy.16.cw = bf16[9,256,64]{2,1,0:T(8,128)(2,1)S(1)} copy(bf16[9,256,64]{1,2,0:T(8,128)(2,1)} %param.16) | data formatting | bytes 589824 | tf_op args[3]
  8.0 0.7 pad.11
  8.6 0.7 pad.12
  10.0 0.9 copy-done.5
  10.9 0.9 copy-done.6
  11.8 1.1 pack_weights.1
  13.0 7.2 %split_rows.1 = (bf16[16,64,512]{2,1,0:T(8,128)(2,1)}, bf16[17,64,256]{2,1,0:T(8,128)(2,1)S(1)}) custom-call(bf16[64,16,4,128]{3,2,1,0:T(4,128)(2,1)S(1)} %copy-done.2), custom_call_target="tpu_custom_call" | custom-call | tf_op jit(solution)/shard_map/split_rows/pallas_call | solution.py:217
  20.2 5.1 %collective-permute-start = (bf16[17,64,256]{2,1,0:T(8,128)(2,1)S(1)}, bf16[17,64,256]{2,1,0:T(8,128)(2,1)S(1)}, u32[]{:S(2)}, u32[]{:S(2)}) collective-permute-start(bf16[17,64,256]{2,1,0:T(8,128)(2,1)S(1)} %get-tuple-element.11.mine), channel_id=1, source_target_pairs={{0,4},{4,8},{8,12},{1,5},{5,9},{9,13},{2,6},{6,10},{10,14},{3,7},{... | collective-permute-start | bytes 1671176 | tf_op jit(solution)/shard_map/ppermute | solution.py:233
  25.3 1.3 %collective-permute-start.1 = (bf16[17,64,256]{2,1,0:T(8,128)(2,1)S(1)}, bf16[17,64,256]{2,1,0:T(8,128)(2,1)S(1)}, u32[]{:S(2)}, u32[]{:S(2)}) collective-permute-start(bf16[17,64,256]{2,1,0:T(8,128)(2,1)S(1)} %get-tuple-element.11.mine), channel_id=1, source_target_pairs={{4,0},{8,4},{12,8},{5,1},{9,5},{13,9},{6,2},{10,6},{14,10},{7,3},{... | collective-permute-start | bytes 1671176 | tf_op jit(solution)/shard_map/ppermute | solution.py:234
  26.7 10.4 %collective-permute-done.below = bf16[17,64,256]{2,1,0:T(8,128)(2,1)S(1)} collective-permute-done((bf16[17,64,256]{2,1,0:T(8,128)(2,1)S(1)}, bf16[17,64,256]{2,1,0:T(8,128)(2,1)S(1)}, u32[]{:S(2)}, u32[]{:S(2)}) %collective-permute-start) | collective-permute-done | bytes 557088 | tf_op jit(solution)/shard_map/ppermute | solution.py:233
  37.1 4.1 %collective-permute-done.1.above = bf16[17,64,256]{2,1,0:T(8,128)(2,1)S(1)} collective-permute-done((bf16[17,64,256]{2,1,0:T(8,128)(2,1)S(1)}, bf16[17,64,256]{2,1,0:T(8,128)(2,1)S(1)}, u32[]{:S(2)}, u32[]{:S(2)}) %collective-permute-start.1) | collective-permute-done | bytes 557088 | tf_op jit(solution)/shard_map/ppermute | solution.py:234
  41.3 1.4 %flux_rows.1 = bf16[1024,128]{1,0:T(8,128)(2,1)} custom-call(bf16[2048,384]{1,0:T(8,128)(2,1)S(1)} %copy-done.1, bf16[384,64]{1,0:T(8,128)(2,1)S(1)} %copy.17.fw), custom_call_target="tpu_custom_call" | custom-call | tf_op jit(solution)/shard_map/flux_rows/pallas_call | solution.py:252
  42.7 3.5 %all-to-all-start = ((bf16[4,4,64,512]{3,2,1,0:T(8,128)(2,1)}), bf16[4,4,64,512]{3,2,1,0:T(8,128)(2,1)S(1)}, u32[]{:S(2)}, u32[]{:S(2)}) async-start(bf16[4,4,64,512]{3,2,1,0:T(8,128)(2,1)} %bitcast), calls=%async_computation | async-start | bytes 2097152 | tf_op jit(solution)/shard_map/all_to_all | solution.py:230
  46.3 1.1 copy-done.4
  47.4 2.9 %halo.1 = bf16[4,9,64,128]{3,2,1,0:T(8,128)(2,1)} custom-call(s32[16,8]{1,0:T(8,128)S(1)} %clamp_select_fusion.near, bf16[17,64,256]{2,1,0:T(8,128)(2,1)S(1)} %collective-permute-done.below, bf16[17,64,256]{2,1,0:T(8,128)(2,1)S(1)} %copy-done.4, bf16[17,64,256]{2,1,0:T(8,128)(2,1)S(1)} %collective-permute-done.1.above), custom_call_target="tpu_custom_call" | custom-call | tf_op jit(solution)/shard_map/halo/pallas_call | solution.py:283
  50.3 10.3 %all-to-all-done.tile = bf16[4,4,64,512]{3,2,1,0:T(8,128)(2,1)S(1)} async-done(((bf16[4,4,64,512]{3,2,1,0:T(8,128)(2,1)}), bf16[4,4,64,512]{3,2,1,0:T(8,128)(2,1)S(1)}, u32[]{:S(2)}, u32[]{:S(2)}) %all-to-all-start) | async-done | bytes 1048608 | tf_op jit(solution)/shard_map/all_to_all | solution.py:230
  60.6 3.5 %all-to-all-start.1 = ((bf16[4,9,64,128]{3,2,1,0:T(8,128)(2,1)}), bf16[4,9,64,128]{3,2,1,0:T(8,128)(2,1)S(1)}, u32[]{:S(2)}, u32[]{:S(2)}) async-start(bf16[4,9,64,128]{3,2,1,0:T(8,128)(2,1)} %halo.1), calls=%async_computation.1 | async-start | bytes 1179648 | tf_op jit(solution)/shard_map/all_to_all | solution.py:295
  64.3 9.3 %all-to-all-done.1.rim = bf16[4,9,64,128]{3,2,1,0:T(8,128)(2,1)S(1)} async-done(((bf16[4,9,64,128]{3,2,1,0:T(8,128)(2,1)}), bf16[4,9,64,128]{3,2,1,0:T(8,128)(2,1)S(1)}, u32[]{:S(2)}, u32[]{:S(2)}) %all-to-all-start.1) | async-done | bytes 589856 | tf_op jit(solution)/shard_map/all_to_all | solution.py:295
  73.6 1.6 %copy-done = bf16[4416,256]{1,0:T(8,128)(2,1)S(1)} copy-done((bf16[4416,256]{1,0:T(8,128)(2,1)S(1)}, bf16[4416,256]{1,0:T(8,128)(2,1)}, u32[]{:S(2)}) %copy-start) | copy-done | bytes 2261016
  75.3 9.2 %block.1 = bf16[4,4,64,512]{3,2,1,0:T(8,128)(2,1)} custom-call(bf16[4,4,64,512]{3,2,1,0:T(8,128)(2,1)S(1)} %all-to-all-done.tile, bf16[4,9,64,128]{3,2,1,0:T(8,128)(2,1)S(1)} %all-to-all-done.1.rim, bf16[4,1104,256]{2,1,0:T(8,128)(2,1)S(1)} %bitcast.8), custom_call_target="tpu_custom_call" | custom-call | tf_op jit(solution)/shard_map/block/pallas_call | solution.py:296
  84.5 3.5 %all-to-all-start.2 = ((bf16[4,4,64,512]{3,2,1,0:T(8,128)(2,1)}), bf16[4,4,64,512]{3,2,1,0:T(8,128)(2,1)S(1)}, u32[]{:S(2)}, u32[]{:S(2)}) async-start(bf16[4,4,64,512]{3,2,1,0:T(8,128)(2,1)} %block.1), calls=%async_computation.2 | async-start | bytes 2097152 | tf_op jit(solution)/shard_map/all_to_all | solution.py:313
  88.0 1.2 %copy-done.8 = bf16[4096,128]{1,0:T(8,128)(2,1)S(1)} copy-done((bf16[4096,128]{1,0:T(8,128)(2,1)S(1)}, bf16[4096,128]{1,0:T(8,128)(2,1)}, u32[]{:S(2)}) %copy-start.8) | copy-done | bytes 1048600
  89.2 15.8 %pick.1.force = bf16[16,64,512]{2,1,0:T(8,128)(2,1)S(1)} custom-call(s32[8192]{0:T(1024)S(1)} %bitcast.11, bf16[4096,128]{1,0:T(8,128)(2,1)S(1)} %copy-done.8, s32[16,1,512]{2,1,0:T(1,128)S(1)} %bitcast.10), custom_call_target="tpu_custom_call" | custom-call | flops 10000000000 | bytes 4000000 | tf_op jit(solution)/shard_map/pick/pallas_call | solution.py:264
  105.1 4.5 %finish.1 = bf16[64,16,4,128]{3,2,1,0:T(4,128)(2,1)} custom-call(bf16[16,64,512]{2,1,0:T(8,128)(2,1)} %get-tuple-element.10.rows, bf16[16,64,512]{2,1,0:T(8,128)(2,1)S(1)} %bitcast.7, bf16[16,64,512]{2,1,0:T(8,128)(2,1)S(1)} %pick.1.force, s32[16,1,512]{2,1,0:T(1,128)S(1)} %bitcast.9, bf16[64,1]{1,0:T(8,128)(2,1)S(1)} %copy.18.scale), custom_call_target="tpu_custom_call" | custom-call | tf_op jit(solution)/shard_map/finish/pallas_call | solution.py:314
  (37 shorter events, 1.2 us)
Async XLA Ops:
  6.5 6.4 %copy-start.2 = (bf16[64,16,4,128]{3,2,1,0:T(4,128)(2,1)S(1)}, bf16[64,16,4,128]{3,2,1,0:T(4,128)(2,1)}, u32[]{:S(2)}) copy-start(bf16[64,16,4,128]{3,2,1,0:T(4,128)(2,1)} %state.1) | copy-start | bytes 3145732
  6.5 34.7 %copy-start.1 = (bf16[2048,384]{1,0:T(8,128)(2,1)S(1)}, bf16[2048,384]{1,0:T(8,128)(2,1)}, u32[]{:S(2)}) copy-start(bf16[2048,384]{1,0:T(8,128)(2,1)} %atm) | copy-start | bytes 4718596
  6.5 67.1 %all-gather.6.cloned.1.call-start = ((), (), s32[]{:S(2)}) async-start(), calls=%async_computation.4 | async-start | bytes 2826240 | tf_op jit(solution)/shard_map/all_gather | solution.py:247
  10.0 0.9 copy-start.5
  10.9 0.9 copy-start.6
  11.8 14.8 %copy-start.9 = (bf16[384,64]{0,1:T(8,128)(2,1)S(1)}, bf16[384,64]{0,1:T(8,128)(2,1)}, u32[]{:S(2)}) copy-start(bf16[384,64]{0,1:T(8,128)(2,1)} %param.15) | copy-start | bytes 147460
  12.9 75.1 %all-gather.4.cloned.1.call-start = ((), (), s32[]{:S(2)}) async-start(), calls=%async_computation.3 | async-start | bytes 1310720 | tf_op jit(solution)/shard_map/all_gather | solution.py:258
  20.2 22.5 %copy-start.3 = (bf16[17,64,256]{2,1,0:T(8,128)(2,1)}, bf16[17,64,256]{2,1,0:T(8,128)(2,1)S(1)}, u32[]{:S(2)}) copy-start(bf16[17,64,256]{2,1,0:T(8,128)(2,1)S(1)} %get-tuple-element.11.mine) | copy-start | bytes 1671172
  20.2 26.0 %copy-start.11 = (s32[16,8]{0,1:T(8,128)S(1)}, s32[16,8]{0,1:T(8,128)}, u32[]{:S(2)}) copy-start(s32[16,8]{0,1:T(8,128)} %param.24) | copy-start | bytes 1540
  20.2 16.9 %collective-permute-start = (bf16[17,64,256]{2,1,0:T(8,128)(2,1)S(1)}, bf16[17,64,256]{2,1,0:T(8,128)(2,1)S(1)}, u32[]{:S(2)}, u32[]{:S(2)}) collective-permute-start(bf16[17,64,256]{2,1,0:T(8,128)(2,1)S(1)} %get-tuple-element.11.mine), channel_id=1, source_target_pairs={{0,4},{4,8},{8,12},{1,5},{5,9},{9,13},{2,6},{6,10},{10,14},{3,7},{... | collective-permute-start | bytes 1671176 | tf_op jit(solution)/shard_map/ppermute | solution.py:233
  25.3 16.0 %collective-permute-start.1 = (bf16[17,64,256]{2,1,0:T(8,128)(2,1)S(1)}, bf16[17,64,256]{2,1,0:T(8,128)(2,1)S(1)}, u32[]{:S(2)}, u32[]{:S(2)}) collective-permute-start(bf16[17,64,256]{2,1,0:T(8,128)(2,1)S(1)} %get-tuple-element.11.mine), channel_id=1, source_target_pairs={{4,0},{8,4},{12,8},{5,1},{9,5},{13,9},{6,2},{10,6},{14,10},{7,3},{... | collective-permute-start | bytes 1671176 | tf_op jit(solution)/shard_map/ppermute | solution.py:234
  42.7 18.0 %all-to-all-start = ((bf16[4,4,64,512]{3,2,1,0:T(8,128)(2,1)}), bf16[4,4,64,512]{3,2,1,0:T(8,128)(2,1)S(1)}, u32[]{:S(2)}, u32[]{:S(2)}) async-start(bf16[4,4,64,512]{3,2,1,0:T(8,128)(2,1)} %bitcast), calls=%async_computation | async-start | bytes 2097152 | tf_op jit(solution)/shard_map/all_to_all | solution.py:230
  46.2 17.9 %copy-start.12 = (bf16[64]{0:T(256)(128)(2,1)S(1)}, bf16[64]{0:T(256)(128)(2,1)}, u32[]{:S(2)}) copy-start(bf16[64]{0:T(256)(128)(2,1)} %param.22) | copy-start | bytes 388
  46.2 18.0 %copy-start.10 = (s32[16,4,128]{2,1,0:T(4,128)S(1)}, s32[16,4,128]{2,1,0:T(4,128)}, u32[]{:S(2)}) copy-start(s32[16,4,128]{2,1,0:T(4,128)} %param.25) | copy-start | bytes 98308
  46.3 1.1 copy-start.4
  60.6 13.0 %all-to-all-start.1 = ((bf16[4,9,64,128]{3,2,1,0:T(8,128)(2,1)}), bf16[4,9,64,128]{3,2,1,0:T(8,128)(2,1)S(1)}, u32[]{:S(2)}, u32[]{:S(2)}) async-start(bf16[4,9,64,128]{3,2,1,0:T(8,128)(2,1)} %halo.1), calls=%async_computation.1 | async-start | bytes 1179648 | tf_op jit(solution)/shard_map/all_to_all | solution.py:295
  73.6 1.6 %copy-start = (bf16[4416,256]{1,0:T(8,128)(2,1)S(1)}, bf16[4416,256]{1,0:T(8,128)(2,1)}, u32[]{:S(2)}) copy-start(bf16[4416,256]{1,0:T(8,128)(2,1)} %all-gather.6.cloned.1.call-done) | copy-start | bytes 6782980
  84.5 20.6 %all-to-all-start.2 = ((bf16[4,4,64,512]{3,2,1,0:T(8,128)(2,1)}), bf16[4,4,64,512]{3,2,1,0:T(8,128)(2,1)S(1)}, u32[]{:S(2)}, u32[]{:S(2)}) async-start(bf16[4,4,64,512]{3,2,1,0:T(8,128)(2,1)} %block.1), calls=%async_computation.2 | async-start | bytes 2097152 | tf_op jit(solution)/shard_map/all_to_all | solution.py:313
  88.0 1.2 %copy-start.8 = (bf16[4096,128]{1,0:T(8,128)(2,1)S(1)}, bf16[4096,128]{1,0:T(8,128)(2,1)}, u32[]{:S(2)}) copy-start(bf16[4096,128]{1,0:T(8,128)(2,1)} %all-gather.4.cloned.1.call-done.table) | copy-start | bytes 3145732
  89.2 15.8 %copy-start.7 = (s32[16,4,128]{2,1,0:T(4,128)S(1)}, s32[16,4,128]{2,1,0:T(4,128)}, u32[]{:S(2)}) copy-start(s32[16,4,128]{2,1,0:T(4,128)} %param.23) | copy-start | bytes 98308
Sparse Core Ops, SparseCore 0:
  13.0 26.1 all-gather.5
  42.8 28.2 all-gather.3

commit v3 on v2

--- a/solution.py
+++ b/solution.py
@@ -31,10 +31,10 @@
 
 
 def pack_weights(cw, vec, iw, ow, out):
-    taps, chan, cl = cw.shape
+    taps, cl, chan = cw.shape
     hl = iw.shape[1]
     for t in range(taps):
-        out[t * cl : (t + 1) * cl, :] = cw[t].astype(F32).T.astype(BF16)
+        out[t * cl : (t + 1) * cl, :] = cw[t]
     base = taps * cl
     out[base : base + hl, :] = iw[...].astype(F32).T.astype(BF16)
     out[base + hl : base + 2 * hl, :] = ow[...]
@@ -42,12 +42,11 @@
 
 
 def flux_rows(atm, fw, out):
-    cl = fw.shape[1]
     rows = out.shape[0]
     w = fw[...]
     parts = []
     for k in range(atm.shape[0] // rows):
-        parts.append(jnp.dot(atm[k * rows : (k + 1) * rows, :], w, preferred_element_type=F32))
+        parts.append(nt(atm[k * rows : (k + 1) * rows, :], w))
     out[...] = jnp.concatenate(parts, axis=1).astype(BF16)
 
 
@@ -76,6 +75,72 @@
             if i == bh - 1:
                 strips[slot, :, bw : 2 * bw] = cells
     strips[last, :, 0:bw] = edge.astype(BF16)
+
+
+def exchange(rows, strips, tile, below, above, send, recv, own):
+    groups = rows.shape[0]
+    sec = lax.axis_size("sec")
+    tiles = lax.axis_size("tile")
+    me = lax.axis_index("chan") * sec + lax.axis_index("sec")
+    t = lax.axis_index("tile")
+    low, high = t > 0, t < tiles - 1
+    mesh = pl.DeviceIdType.MESH
+
+    def at(p):
+        return {"chan": p // sec, "sec": lax.rem(p, sec)}
+
+    barrier = pltpu.get_barrier_semaphore()
+    for d in range(1, groups):
+        pl.semaphore_signal(
+            barrier, inc=1, device_id=at(lax.rem(me + d, groups)), device_id_type=mesh
+        )
+
+    for step in (1, tiles - 1):
+        pl.semaphore_signal(
+            barrier, inc=1, device_id={"tile": lax.rem(t + step, tiles)}, device_id_type=mesh
+        )
+    pl.semaphore_wait(barrier, groups + 1)
+
+    def strip(k, dst, to):
+        return pltpu.make_async_remote_copy(
+            src_ref=strips, dst_ref=dst, send_sem=send.at[groups + k], recv_sem=recv.at[groups + k],
+            device_id={"tile": to}, device_id_type=mesh,
+        )
+
+    up, down = strip(0, below, t + 1), strip(1, above, t - 1)
+
+    @pl.when(high)
+    def _():
+        up.start()
+
+    @pl.when(low)
+    def _():
+        down.start()
+
+    copies = []
+    for d in range(1, groups):
+        to = lax.rem(me + d, groups)
+        copy = pltpu.make_async_remote_copy(
+            src_ref=rows.at[to], dst_ref=tile.at[me], send_sem=send.at[d], recv_sem=recv.at[d],
+            device_id=at(to), device_id_type=mesh,
+        )
+        copy.start()
+        copies.append(copy)
+    mine = pltpu.make_async_copy(rows.at[me], tile.at[me], own)
+    mine.start()
+    mine.wait()
+    for copy in copies:
+        copy.wait()
+
+    @pl.when(high)
+    def _():
+        up.wait_send()
+        down.wait_recv()
+
+    @pl.when(low)
+    def _():
+        down.wait_send()
+        up.wait_recv()
 
 
 def halo(near, below, mine, above, out, *, per):
@@ -227,25 +292,38 @@
         compiler_params=params(),
         name="split_rows",
     )(ocean_state)
-    tile = lax.all_to_all(
-        rows.reshape(groups, per, cl, cells), ("chan", "sec"), split_axis=0, concat_axis=0
-    )
-    below = lax.ppermute(strips, "tile", [(i, i + 1) for i in range(tiles - 1)])
-    above = lax.ppermute(strips, "tile", [(i + 1, i) for i in range(tiles - 1)])
-
     vec = jnp.stack(
         [jnp.pad(v, (0, chan - v.shape[0])) for v in (in_bias, conv_bias, norm_gain)]
     )
     vec = jnp.pad(vec, ((0, 13), (0, 0)))
     pack_rows = 9 * cl + 2 * hl + 16
-    pack = pl.pallas_call(
+    pack_local = pl.pallas_call(
         pack_weights,
         out_shape=jax.ShapeDtypeStruct((pack_rows, chan), BF16),
         compiler_params=params(),
         name="pack_weights",
-    )(conv_weight, vec, in_weight, out_weight)
-    pack = lax.all_gather(pack, ("chan", "sec"), axis=0)
-
+    )(jnp.swapaxes(conv_weight, 1, 2), vec, in_weight, out_weight)
+    pack = lax.all_gather(pack_local, ("chan", "sec"), axis=0)
+
+    rows, strips, _ = lax.optimization_barrier((rows, strips, pack_local))
+    anywhere = pl.BlockSpec(memory_space=pl.ANY)
+    tile, below, above = pl.pallas_call(
+        exchange,
+        in_specs=[anywhere, anywhere],
+        out_specs=[anywhere] * 3,
+        out_shape=[
+            jax.ShapeDtypeStruct((groups, per, cl, cells), BF16),
+            jax.ShapeDtypeStruct(strips.shape, BF16),
+            jax.ShapeDtypeStruct(strips.shape, BF16),
+        ],
+        scratch_shapes=[
+            pltpu.SemaphoreType.DMA((groups + 2,)),
+            pltpu.SemaphoreType.DMA((groups + 2,)),
+            pltpu.SemaphoreType.DMA,
+        ],
+        compiler_params=pltpu.CompilerParams(collective_id=0, has_side_effects=True),
+        name="exchange",
+    )(rows.reshape(groups, per, cl, cells), strips)
     below, above, atmos = lax.optimization_barrier((below, above, atmos))
     parts = 128 // cl
     trows = atmos.shape[0] // parts
@@ -254,7 +332,7 @@
         out_shape=jax.ShapeDtypeStruct((trows, 128), BF16),
         compiler_params=params(),
         name="flux_rows",
-    )(atmos, flux_weight)
+    )(atmos, flux_weight.T)
     table = lax.all_gather(table, "tile", axis=0, tiled=True)
 
     local = lax.rem(remap, trows * parts)

time: 117 us -> 107 us (0.915)
  waiting for transfers between devices: 34.2 us -> 10.5 us
  Pallas kernels: 42.1 us -> 65.6 us
  starting transfers between devices: 16.9 us -> 7.03 us
    pallas_call x0 -> x1, Pallas kernels: none -> 25.6 us  [on_device(): pl.pallas_call(exchange, in_specs=[anywhere, anywhere], out_specs=[anywhe...]
    ppermute x2 -> x0, waiting for transfers between devices: 14.5 us -> none  [the longest x1 10.4 us: on_device(): below = lax.ppermute(strips, 'tile', [(i, i + 1) for i in range(tiles - 1)])]
    all_to_all x1 -> x0, waiting for transfers between devices: 10.3 us -> none  [on_device(): lax.all_to_all(rows.reshape(groups, per, cl, cells), ('chan', 'sec'), spl...]
    ppermute x2 -> x0, starting transfers between devices: 6.37 us -> none  [the longest x1 5.08 us: on_device(): below = lax.ppermute(strips, 'tile', [(i, i + 1) for i in range(tiles - 1)])]
    all_to_all x1 -> x0, starting transfers between devices: 3.53 us -> none  [on_device(): lax.all_to_all(rows.reshape(groups, per, cl, cells), ('chan', 'sec'), spl...]
    pallas_call x1, Pallas kernels: 4.45 us -> 3.17 us  [on_device(): pl.pallas_call(finish, grid=(slots // some,), in_specs=[some_spec, some_s...]
    unnamed x29 -> x39, local copies, waits for them, and re-layouts: 7.37 us -> 7.53 us
  transfers between devices with their start and end apart: 7 -> 4, of which waited for: 4 -> 2; matrix products, arithmetic and copies ran while one was open for 0% -> 0% of each run, Pallas kernels for 31% -> 58%
where the time goes in v3:
time: 107 us
  Pallas kernels  65.6 us (61%)
  between operations  13.6 us (13%)
  waiting for transfers between devices  10.5 us (10%)
  local copies, waits for them, and re-layouts  9.78 us (9%)
  starting transfers between devices  7.03 us (7%)
    pallas_call x1, Pallas kernels, on_device(): pl.pallas_call(exchange, in_specs=[anywhere, anywhere], out_specs=[anywhe...  25.6 us
    pallas_call x1, Pallas kernels, on_device(): pl.pallas_call(functools.partial(pick, cl=cl), grid_spec=pltpu.PrefetchSc...  15.8 us
    all_to_all x1, waiting for transfers between devices, on_device(): rim = lax.all_to_all(rim, ('chan', 'sec'), split_axis=0, concat_axis=0)  9.43 us
    pallas_call x1, Pallas kernels, on_device(): pl.pallas_call(functools.partial(block, hl=hl), grid=(per,), in_specs=[pl...  9.18 us
    unnamed x39, local copies, waits for them, and re-layouts  7.53 us
    pallas_call x1, Pallas kernels, on_device(): pl.pallas_call(split_rows, grid=(slots // some,), in_specs=[state_spec],...  6.62 us
    all_to_all x1, starting transfers between devices, on_device(): lax.all_to_all(update, ('chan', 'sec'), split_axis=0, concat_axis=0)  3.51 us
    all_to_all x1, starting transfers between devices, on_device(): rim = lax.all_to_all(rim, ('chan', 'sec'), split_axis=0, concat_axis=0)  3.48 us
  transfers between devices with their start and end apart: 4, of which 2 were waited for; matrix products, arithmetic and copies ran while one was open for 0% of the time, Pallas kernels for 58%

profile of v3, /device:TPU:0, one launch (start us, length us, event | category | flops | bytes accessed | tf_op | source)
XLA Modules:
  0.0 106.7 jit_solution(14202212661760886262)
XLA Ops:
  6.5 0.8 pad.11
  7.4 0.7 pad.12
  8.0 0.7 stack.12
  8.7 1.0 copy-done.10
  9.7 0.9 copy-done.11
  10.6 0.9 copy-done.12
  11.5 0.9 pack_weights.1
  12.5 6.6 %split_rows.1 = (bf16[16,64,512]{2,1,0:T(8,128)(2,1)S(1)}, bf16[17,64,256]{2,1,0:T(8,128)(2,1)S(1)}) custom-call(bf16[64,16,4,128]{3,2,1,0:T(4,128)(2,1)S(1)} %copy-done.7), custom_call_target="tpu_custom_call" | custom-call | tf_op jit(solution)/shard_map/split_rows/pallas_call | solution.py:282
  19.1 1.0 copy-done
  20.1 0.8 copy-done.3
  20.9 25.6 %exchange.1 = (bf16[4,4,64,512]{3,2,1,0:T(8,128)(2,1)}, bf16[17,64,256]{2,1,0:T(8,128)(2,1)}, bf16[17,64,256]{2,1,0:T(8,128)(2,1)}) custom-call(bf16[4,4,64,512]{3,2,1,0:T(8,128)(2,1)} %bitcast.9, bf16[17,64,256]{2,1,0:T(8,128)(2,1)} %copy-done.3), custom_call_target="tpu_custom_call" | custom-call | tf_op jit(solution)/shard_map/exchange/pallas_call | solution.py:310
  46.6 1.3 %flux_rows.1 = bf16[1024,128]{1,0:T(8,128)(2,1)} custom-call(bf16[2048,384]{1,0:T(8,128)(2,1)S(1)} %copy-done.5, bf16[64,384]{1,0:T(8,128)(2,1)S(1)} %bitcast.13), custom_call_target="tpu_custom_call" | custom-call | tf_op jit(solution)/shard_map/flux_rows/pallas_call | solution.py:330
  48.1 2.9 %halo.1 = bf16[4,9,64,128]{3,2,1,0:T(8,128)(2,1)} custom-call(s32[16,8]{1,0:T(8,128)S(1)} %clamp_select_fusion.near, bf16[17,64,256]{2,1,0:T(8,128)(2,1)S(1)} %copy-done.8, bf16[17,64,256]{2,1,0:T(8,128)(2,1)S(1)} %copy-done.4, bf16[17,64,256]{2,1,0:T(8,128)(2,1)S(1)} %copy-done.9), custom_call_target="tpu_custom_call" | custom-call | tf_op jit(solution)/shard_map/halo/pallas_call | solution.py:361
  51.0 3.5 %all-to-all-start = ((bf16[4,9,64,128]{3,2,1,0:T(8,128)(2,1)}), bf16[4,9,64,128]{3,2,1,0:T(8,128)(2,1)S(1)}, u32[]{:S(2)}, u32[]{:S(2)}) async-start(bf16[4,9,64,128]{3,2,1,0:T(8,128)(2,1)} %halo.1), calls=%async_computation | async-start | bytes 1179648 | tf_op jit(solution)/shard_map/all_to_all | solution.py:373
  54.5 0.1 copy.16.scale
  54.6 0.1 add_select_fusion
  54.7 9.4 %all-to-all-done.rim = bf16[4,9,64,128]{3,2,1,0:T(8,128)(2,1)S(1)} async-done(((bf16[4,9,64,128]{3,2,1,0:T(8,128)(2,1)}), bf16[4,9,64,128]{3,2,1,0:T(8,128)(2,1)S(1)}, u32[]{:S(2)}, u32[]{:S(2)}) %all-to-all-start) | async-done | bytes 589856 | tf_op jit(solution)/shard_map/all_to_all | solution.py:373
  64.1 1.6 %copy-done.2 = bf16[4416,256]{1,0:T(8,128)(2,1)S(1)} copy-done((bf16[4416,256]{1,0:T(8,128)(2,1)S(1)}, bf16[4416,256]{1,0:T(8,128)(2,1)}, u32[]{:S(2)}) %copy-start.2) | copy-done | bytes 2261016
  65.8 9.2 %block.1 = bf16[4,4,64,512]{3,2,1,0:T(8,128)(2,1)} custom-call(bf16[4,4,64,512]{3,2,1,0:T(8,128)(2,1)S(1)} %copy-done.6, bf16[4,9,64,128]{3,2,1,0:T(8,128)(2,1)S(1)} %all-to-all-done.rim, bf16[4,1104,256]{2,1,0:T(8,128)(2,1)S(1)} %bitcast.11), custom_call_target="tpu_custom_call" | custom-call | tf_op jit(solution)/shard_map/block/pallas_call | solution.py:374
  75.0 3.5 %all-to-all-start.1 = ((bf16[4,4,64,512]{3,2,1,0:T(8,128)(2,1)}), bf16[4,4,64,512]{3,2,1,0:T(8,128)(2,1)S(1)}, u32[]{:S(2)}, u32[]{:S(2)}) async-start(bf16[4,4,64,512]{3,2,1,0:T(8,128)(2,1)} %block.1), calls=%async_computation.1 | async-start | bytes 2097152 | tf_op jit(solution)/shard_map/all_to_all | solution.py:391
  78.5 1.1 %all-gather.4.cloned.1.call-done.table = bf16[4096,128]{1,0:T(8,128)(2,1)} async-done(((bf16[1024,128]{1,0:T(8,128)(2,1)}), bf16[4096,128]{1,0:T(8,128)(2,1)}) %all-gather.4.cloned.1.call-update) | async-done | bytes 1048592 | tf_op jit(solution)/shard_map/all_gather | solution.py:336
  79.6 1.2 %copy-done.15 = bf16[4096,128]{1,0:T(8,128)(2,1)S(1)} copy-done((bf16[4096,128]{1,0:T(8,128)(2,1)S(1)}, bf16[4096,128]{1,0:T(8,128)(2,1)}, u32[]{:S(2)}) %copy-start.15) | copy-done | bytes 1048600
  80.8 15.8 %pick.1.force = bf16[16,64,512]{2,1,0:T(8,128)(2,1)S(1)} custom-call(s32[8192]{0:T(1024)S(1)} %bitcast.16, bf16[4096,128]{1,0:T(8,128)(2,1)S(1)} %copy-done.15, s32[16,1,512]{2,1,0:T(1,128)S(1)} %bitcast.15), custom_call_target="tpu_custom_call" | custom-call | flops 10000000000 | bytes 4000000 | tf_op jit(solution)/shard_map/pick/pallas_call | solution.py:342
  96.6 3.2 %finish.1 = bf16[64,16,4,128]{3,2,1,0:T(4,128)(2,1)} custom-call(bf16[16,64,512]{2,1,0:T(8,128)(2,1)S(1)} %copy-done.1, bf16[16,64,512]{2,1,0:T(8,128)(2,1)S(1)} %bitcast.10, bf16[16,64,512]{2,1,0:T(8,128)(2,1)S(1)} %pick.1.force, s32[16,1,512]{2,1,0:T(1,128)S(1)} %bitcast.14, bf16[64,1]{1,0:T(8,128)(2,1)S(1)} %copy.16.scale), custom_call_target="tpu_custom_call" | custom-call | tf_op jit(solution)/shard_map/finish/pallas_call | solution.py:392
  (42 shorter events, 0.3 us)
Async XLA Ops:
  6.5 5.9 %copy-start.7 = (bf16[64,16,4,128]{3,2,1,0:T(4,128)(2,1)S(1)}, bf16[64,16,4,128]{3,2,1,0:T(4,128)(2,1)}, u32[]{:S(2)}) copy-start(bf16[64,16,4,128]{3,2,1,0:T(4,128)(2,1)} %state.1) | copy-start | bytes 3145732
  6.5 40.0 %copy-start.5 = (bf16[2048,384]{1,0:T(8,128)(2,1)S(1)}, bf16[2048,384]{1,0:T(8,128)(2,1)}, u32[]{:S(2)}) copy-start(bf16[2048,384]{1,0:T(8,128)(2,1)} %atm) | copy-start | bytes 4718596
  6.5 57.6 %all-gather.6.cloned.1.call-start = ((), (), s32[]{:S(2)}) async-start(), calls=%async_computation.3 | async-start | bytes 2826240 | tf_op jit(solution)/shard_map/all_gather | solution.py:306
  8.7 1.0 copy-start.10
  9.7 0.9 copy-start.11
  10.6 0.9 copy-start.12
  11.5 35.1 %copy-start.13 = (bf16[384,64]{0,1:T(8,128)(2,1)S(1)}, bf16[384,64]{0,1:T(8,128)(2,1)}, u32[]{:S(2)}) copy-start(bf16[384,64]{0,1:T(8,128)(2,1)} %param.15) | copy-start | bytes 147460
  12.4 35.5 %copy-start.17 = (s32[16,8]{0,1:T(8,128)S(1)}, s32[16,8]{0,1:T(8,128)}, u32[]{:S(2)}) copy-start(s32[16,8]{0,1:T(8,128)} %param.24) | copy-start | bytes 1540
  12.4 67.1 %all-gather.4.cloned.1.call-start = ((), (), s32[]{:S(2)}) async-start(), calls=%async_computation.2 | async-start | bytes 1310720 | tf_op jit(solution)/shard_map/all_gather | solution.py:336
  19.1 1.0 copy-start
  20.1 0.8 copy-start.3
  20.9 27.1 %copy-start.4 = (bf16[17,64,256]{2,1,0:T(8,128)(2,1)S(1)}, bf16[17,64,256]{2,1,0:T(8,128)(2,1)}, u32[]{:S(2)}) copy-start(bf16[17,64,256]{2,1,0:T(8,128)(2,1)} %copy-done.3) | copy-start | bytes 1671172
  46.6 1.5 %copy-start.8 = (bf16[17,64,256]{2,1,0:T(8,128)(2,1)S(1)}, bf16[17,64,256]{2,1,0:T(8,128)(2,1)}, u32[]{:S(2)}) copy-start(bf16[17,64,256]{2,1,0:T(8,128)(2,1)} %get-tuple-element.22.below) | copy-start | bytes 1671172
  46.6 1.5 %copy-start.9 = (bf16[17,64,256]{2,1,0:T(8,128)(2,1)S(1)}, bf16[17,64,256]{2,1,0:T(8,128)(2,1)}, u32[]{:S(2)}) copy-start(bf16[17,64,256]{2,1,0:T(8,128)(2,1)} %get-tuple-element.23.above) | copy-start | bytes 1671172
  47.9 6.6 %copy-start.18 = (bf16[64]{0:T(256)(128)(2,1)S(1)}, bf16[64]{0:T(256)(128)(2,1)}, u32[]{:S(2)}) copy-start(bf16[64]{0:T(256)(128)(2,1)} %param.22) | copy-start | bytes 388
  47.9 6.7 %copy-start.16 = (s32[16,4,128]{2,1,0:T(4,128)S(1)}, s32[16,4,128]{2,1,0:T(4,128)}, u32[]{:S(2)}) copy-start(s32[16,4,128]{2,1,0:T(4,128)} %param.25) | copy-start | bytes 98308
  47.9 16.2 %copy-start.6 = (bf16[4,4,64,512]{3,2,1,0:T(8,128)(2,1)S(1)}, bf16[4,4,64,512]{3,2,1,0:T(8,128)(2,1)}, u32[]{:S(2)}) copy-start(bf16[4,4,64,512]{3,2,1,0:T(8,128)(2,1)} %get-tuple-element.19.tile) | copy-start | bytes 3145732
  51.0 13.1 %all-to-all-start = ((bf16[4,9,64,128]{3,2,1,0:T(8,128)(2,1)}), bf16[4,9,64,128]{3,2,1,0:T(8,128)(2,1)S(1)}, u32[]{:S(2)}, u32[]{:S(2)}) async-start(bf16[4,9,64,128]{3,2,1,0:T(8,128)(2,1)} %halo.1), calls=%async_computation | async-start | bytes 1179648 | tf_op jit(solution)/shard_map/all_to_all | solution.py:373
  64.1 1.6 %copy-start.2 = (bf16[4416,256]{1,0:T(8,128)(2,1)S(1)}, bf16[4416,256]{1,0:T(8,128)(2,1)}, u32[]{:S(2)}) copy-start(bf16[4416,256]{1,0:T(8,128)(2,1)} %all-gather.6.cloned.1.call-done) | copy-start | bytes 6782980
  75.0 21.7 %all-to-all-start.1 = ((bf16[4,4,64,512]{3,2,1,0:T(8,128)(2,1)}), bf16[4,4,64,512]{3,2,1,0:T(8,128)(2,1)S(1)}, u32[]{:S(2)}, u32[]{:S(2)}) async-start(bf16[4,4,64,512]{3,2,1,0:T(8,128)(2,1)} %block.1), calls=%async_computation.1 | async-start | bytes 2097152 | tf_op jit(solution)/shard_map/all_to_all | solution.py:391
  79.6 1.2 %copy-start.15 = (bf16[4096,128]{1,0:T(8,128)(2,1)S(1)}, bf16[4096,128]{1,0:T(8,128)(2,1)}, u32[]{:S(2)}) copy-start(bf16[4096,128]{1,0:T(8,128)(2,1)} %all-gather.4.cloned.1.call-done.table) | copy-start | bytes 3145732
  80.8 15.8 %copy-start.1 = (bf16[16,64,512]{2,1,0:T(8,128)(2,1)S(1)}, bf16[16,64,512]{2,1,0:T(8,128)(2,1)}, u32[]{:S(2)}) copy-start(bf16[16,64,512]{2,1,0:T(8,128)(2,1)} %copy-done) | copy-start | bytes 3145732
  80.8 15.9 %copy-start.14 = (s32[16,4,128]{2,1,0:T(4,128)S(1)}, s32[16,4,128]{2,1,0:T(4,128)}, u32[]{:S(2)}) copy-start(s32[16,4,128]{2,1,0:T(4,128)} %param.23) | copy-start | bytes 98308
Sparse Core Ops, SparseCore 0:
  12.5 35.2 all-gather.5
  49.4 30.1 all-gather.3

commit v4 on v3

--- a/solution.py
+++ b/solution.py
@@ -77,7 +77,7 @@
     strips[last, :, 0:bw] = edge.astype(BF16)
 
 
-def exchange(rows, strips, tile, below, above, send, recv, own):
+def exchange(rows, strips, pack, tile, below, above, packs, send, recv, wsend, wrecv, own):
     groups = rows.shape[0]
     sec = lax.axis_size("sec")
     tiles = lax.axis_size("tile")
@@ -117,6 +117,23 @@
     def _():
         down.start()
 
+    chans = lax.axis_size("chan")
+    c, k = lax.axis_index("chan"), lax.axis_index("sec")
+
+    def weights(src, slot, i, to):
+        copy = pltpu.make_async_remote_copy(
+            src_ref=src, dst_ref=packs.at[slot], send_sem=wsend.at[i], recv_sem=wrecv.at[i],
+            device_id=to, device_id_type=mesh,
+        )
+        copy.start()
+        return copy
+
+    level = [
+        weights(pack, me, d, {"chan": lax.rem(c + d, chans)}) for d in range(1, chans)
+    ]
+    passed = [
+        weights(pack, me, e * chans, {"sec": lax.rem(k + e, sec)}) for e in range(1, sec)
+    ]
     copies = []
     for d in range(1, groups):
         to = lax.rem(me + d, groups)
@@ -126,9 +143,23 @@
         )
         copy.start()
         copies.append(copy)
-    mine = pltpu.make_async_copy(rows.at[me], tile.at[me], own)
+    mine = pltpu.make_async_copy(rows.at[me], tile.at[me], own.at[0])
     mine.start()
+    held = pltpu.make_async_copy(pack, packs.at[me], own.at[1])
+    held.start()
+    for d in range(1, chans):
+        level[d - 1].wait_recv()
+        slot = lax.rem(c - d + chans, chans) * sec + k
+        for e in range(1, sec):
+            passed.append(
+                weights(packs.at[slot], slot, e * chans + d, {"sec": lax.rem(k + e, sec)})
+            )
     mine.wait()
+    held.wait()
+    for copy in level:
+        copy.wait_send()
+    for copy in passed:
+        copy.wait()
     for copy in copies:
         copy.wait()
 
@@ -252,12 +283,14 @@
     out[0] = total.astype(BF16)
 
 
-def finish(rows, update, force, mask, scale, out, scr):
+def finish(rows, update, early, late, mask, scale, out, scr):
     cl, some, bh, bw = out.shape
     gain = scale[:, 0:1].astype(F32)
+    first = pl.program_id(0) < pl.num_programs(0) // 2
     for j in range(some):
         total = rows[j].astype(F32) + gain * update[j].astype(F32)
-        total = (total + force[j].astype(F32)) * mask[j].astype(F32)
+        force = jnp.where(first, early[j].astype(F32), late[j].astype(F32))
+        total = (total + force) * mask[j].astype(F32)
         for i in range(bh):
             scr[:, i, :] = total[:, i * bw : (i + 1) * bw]
         out[:, j] = scr[...].astype(BF16)
@@ -303,28 +336,7 @@
         compiler_params=params(),
         name="pack_weights",
     )(jnp.swapaxes(conv_weight, 1, 2), vec, in_weight, out_weight)
-    pack = lax.all_gather(pack_local, ("chan", "sec"), axis=0)
-
-    rows, strips, _ = lax.optimization_barrier((rows, strips, pack_local))
-    anywhere = pl.BlockSpec(memory_space=pl.ANY)
-    tile, below, above = pl.pallas_call(
-        exchange,
-        in_specs=[anywhere, anywhere],
-        out_specs=[anywhere] * 3,
-        out_shape=[
-            jax.ShapeDtypeStruct((groups, per, cl, cells), BF16),
-            jax.ShapeDtypeStruct(strips.shape, BF16),
-            jax.ShapeDtypeStruct(strips.shape, BF16),
-        ],
-        scratch_shapes=[
-            pltpu.SemaphoreType.DMA((groups + 2,)),
-            pltpu.SemaphoreType.DMA((groups + 2,)),
-            pltpu.SemaphoreType.DMA,
-        ],
-        compiler_params=pltpu.CompilerParams(collective_id=0, has_side_effects=True),
-        name="exchange",
-    )(rows.reshape(groups, per, cl, cells), strips)
-    below, above, atmos = lax.optimization_barrier((below, above, atmos))
+
     parts = 128 // cl
     trows = atmos.shape[0] // parts
     table = pl.pallas_call(
@@ -333,26 +345,49 @@
         compiler_params=params(),
         name="flux_rows",
     )(atmos, flux_weight.T)
+    rows, strips, pack_local, table = lax.optimization_barrier((rows, strips, pack_local, table))
     table = lax.all_gather(table, "tile", axis=0, tiled=True)
 
+    anywhere = pl.BlockSpec(memory_space=pl.ANY)
+    tile, below, above, pack = pl.pallas_call(
+        exchange,
+        in_specs=[anywhere] * 3,
+        out_specs=[anywhere] * 4,
+        out_shape=[
+            jax.ShapeDtypeStruct((groups, per, cl, cells), BF16),
+            jax.ShapeDtypeStruct(strips.shape, BF16),
+            jax.ShapeDtypeStruct(strips.shape, BF16),
+            jax.ShapeDtypeStruct((groups, pack_rows, chan), BF16),
+        ],
+        scratch_shapes=[
+            pltpu.SemaphoreType.DMA((groups + 2,)),
+            pltpu.SemaphoreType.DMA((groups + 2,)),
+            pltpu.SemaphoreType.DMA((groups,)),
+            pltpu.SemaphoreType.DMA((groups,)),
+            pltpu.SemaphoreType.DMA((2,)),
+        ],
+        compiler_params=pltpu.CompilerParams(collective_id=0, has_side_effects=True),
+        name="exchange",
+    )(rows.reshape(groups, per, cl, cells), strips, pack_local)
     local = lax.rem(remap, trows * parts)
     flat = (remap // (trows * parts)) * trows + lax.rem(local, trows)
     which = (local // trows).reshape(slots, 1, cells)
     lane_spec = pl.BlockSpec((1, 1, cells), lambda s, *_: (s, 0, 0))
-    forcing = pl.pallas_call(
+    picks = pl.pallas_call(
         functools.partial(pick, cl=cl),
         grid_spec=pltpu.PrefetchScalarGridSpec(
             num_scalar_prefetch=1,
-            grid=(slots,),
+            grid=(slots // 2,),
             in_specs=[whole(tiles * trows, 128), lane_spec],
             out_specs=slot_spec,
             scratch_shapes=[pltpu.VMEM((tiles * trows, 128), F32), pltpu.VMEM((cells, 128), F32)],
         ),
-        out_shape=jax.ShapeDtypeStruct((slots, cl, cells), BF16),
-        compiler_params=params(),
-        cost_estimate=pl.CostEstimate(flops=10**10, bytes_accessed=4 * 10**6, transcendentals=0),
+        out_shape=jax.ShapeDtypeStruct((slots // 2, cl, cells), BF16),
+        compiler_params=params(),
+        cost_estimate=pl.CostEstimate(flops=5 * 10**9, bytes_accessed=4 * 10**6, transcendentals=0),
         name="pick",
-    )(flat.reshape(-1), table, which)
+    )
+    flat, half = flat.reshape(2, -1), slots // 2
 
     first = (lax.axis_index("tile") - 1) * slots
     near = jnp.where(neighbours >= 0, jnp.clip(neighbours - first, 0, 3 * slots - 1), -1)
@@ -370,7 +405,10 @@
         compiler_params=params(),
         name="halo",
     )(near, below, strips, above)
+    early, rim = lax.optimization_barrier((flat[0], rim))
+    early = picks(early, table, which[:half])
     rim = lax.all_to_all(rim, ("chan", "sec"), split_axis=0, concat_axis=0)
+    early, tile = lax.optimization_barrier((early, tile))
     update = pl.pallas_call(
         functools.partial(block, hl=hl),
         grid=(per,),
@@ -388,12 +426,17 @@
         compiler_params=params(),
         name="block",
     )(tile, rim, pack)
+    late, update = lax.optimization_barrier((flat[1], update))
+    late = picks(late, table, which[half:])
     update = lax.all_to_all(update, ("chan", "sec"), split_axis=0, concat_axis=0)
+    last = half // some - 1
     return pl.pallas_call(
         finish,
         grid=(slots // some,),
         in_specs=[
-            some_spec, some_spec, some_spec,
+            some_spec, some_spec,
+            pl.BlockSpec((some, cl, cells), lambda s: (jnp.minimum(s, last), 0, 0)),
+            pl.BlockSpec((some, cl, cells), lambda s: (jnp.maximum(s - last - 1, 0), 0, 0)),
             pl.BlockSpec((some, 1, cells), lambda s: (s, 0, 0)), whole(cl, 1),
         ],
         out_specs=state_spec,
@@ -404,7 +447,8 @@
     )(
         rows,
         update.reshape(slots, cl, cells),
-        forcing,
+        early,
+        late,
         cell_mask.reshape(slots, 1, cells),
         layer_scale.reshape(cl, 1),
     )

time: 107 us -> 112 us (1.047)
  Pallas kernels: 65.6 us -> 71.3 us
  waiting for transfers between devices: 10.5 us -> 4.85 us
  local copies, waits for them, and re-layouts: 9.78 us -> 14 us
    all_to_all x1, waiting for transfers between devices: 9.43 us -> 0.01 us  [on_device(): rim = lax.all_to_all(rim, ('chan', 'sec'), split_axis=0, concat_axis=0)]
    pallas_call x2 -> x3, Pallas kernels: 41.5 us -> 48 us  [the longest x1 31.5 us: on_device(): pl.pallas_call(exchange, in_specs=[anywhere] * 3, out_specs=[anywhere] *...]
    all_to_all x1, waiting for transfers between devices: 0.01 us -> 4.81 us  [on_device(): lax.all_to_all(update, ('chan', 'sec'), split_axis=0, concat_axis=0)]
    unnamed x39 -> x43, local copies, waits for them, and re-layouts: 7.53 us -> 11.9 us
  transfers between devices with their start and end apart: 4 -> 3, of which waited for: 2 -> 1; matrix products, arithmetic and copies ran while one was open for 0% -> 0% of each run, Pallas kernels for 58% -> 46%
where the time goes in v4:
time: 112 us; the launch traced here: 111 us
  Pallas kernels  71.3 us (64%)
  local copies, waits for them, and re-layouts  14 us (12%)
  between operations  13.6 us (12%)
  starting transfers between devices  7 us (6%)
  waiting for transfers between devices  4.85 us (4%)
    pallas_call x1, Pallas kernels, on_device(): pl.pallas_call(exchange, in_specs=[anywhere] * 3, out_specs=[anywhere] *...  31.5 us
    unnamed x43, local copies, waits for them, and re-layouts  11.9 us
    pallas_call x1, Pallas kernels, on_device(): pl.pallas_call(functools.partial(block, hl=hl), grid=(per,), in_specs=[pl...  9.18 us
    pallas_call x1, Pallas kernels, on_device(): early = picks(early, table, which[:half])  8.25 us
    pallas_call x1, Pallas kernels, on_device(): late = picks(late, table, which[half:])  8.25 us
    pallas_call x1, Pallas kernels, on_device(): pl.pallas_call(split_rows, grid=(slots // some,), in_specs=[state_spec],...  6.62 us
    all_to_all x1, waiting for transfers between devices, on_device(): lax.all_to_all(update, ('chan', 'sec'), split_axis=0, concat_axis=0)  4.81 us
    all_to_all x1, starting transfers between devices, on_device(): lax.all_to_all(update, ('chan', 'sec'), split_axis=0, concat_axis=0)  3.51 us
  transfers between devices with their start and end apart: 3, of which 1 were waited for; matrix products, arithmetic and copies ran while one was open for 0% of the time, Pallas kernels for 46%

profile of v4, /device:TPU:0, one launch (start us, length us, event | category | flops | bytes accessed | tf_op | source)
XLA Modules:
  0.0 110.9 jit_solution(15782728968690697712)
XLA Ops:
  6.5 1.2 %copy-done.8 = bf16[64,16,4,128]{3,2,1,0:T(4,128)(2,1)S(1)} copy-done((bf16[64,16,4,128]{3,2,1,0:T(4,128)(2,1)S(1)}, bf16[64,16,4,128]{3,2,1,0:T(4,128)(2,1)}, u32[]{:S(2)}) %copy-start.8) | copy-done | bytes 1048600
  7.8 6.6 %split_rows.1 = (bf16[16,64,512]{2,1,0:T(8,128)(2,1)S(1)}, bf16[17,64,256]{2,1,0:T(8,128)(2,1)S(1)}) custom-call(bf16[64,16,4,128]{3,2,1,0:T(4,128)(2,1)S(1)} %copy-done.8), custom_call_target="tpu_custom_call" | custom-call | tf_op jit(solution)/shard_map/split_rows/pallas_call | solution.py:315
  14.4 1.0 copy-done
  15.4 0.8 copy-done.4
  16.2 0.7 pad.11
  16.9 0.7 pad.12
  18.2 1.4 %copy-done.6 = bf16[2048,384]{1,0:T(8,128)(2,1)S(1)} copy-done((bf16[2048,384]{1,0:T(8,128)(2,1)S(1)}, bf16[2048,384]{1,0:T(8,128)(2,1)}, u32[]{:S(2)}) %copy-start.6) | copy-done | bytes 1572888
  19.6 0.8 copy-done.14
  20.4 1.3 %flux_rows.1 = bf16[1024,128]{1,0:T(8,128)(2,1)} custom-call(bf16[2048,384]{1,0:T(8,128)(2,1)S(1)} %copy-done.6, bf16[64,384]{1,0:T(8,128)(2,1)S(1)} %bitcast.13), custom_call_target="tpu_custom_call" | custom-call | tf_op jit(solution)/shard_map/flux_rows/pallas_call | solution.py:342
  21.9 0.8 copy-done.3
  22.9 31.5 %exchange.1 = (bf16[4,4,64,512]{3,2,1,0:T(8,128)(2,1)}, bf16[17,64,256]{2,1,0:T(8,128)(2,1)}, bf16[17,64,256]{2,1,0:T(8,128)(2,1)}, bf16[4,1104,256]{2,1,0:T(8,128)(2,1)}) custom-call(bf16[4,4,64,512]{3,2,1,0:T(8,128)(2,1)} %bitcast.10, bf16[17,64,256]{2,1,0:T(8,128)(2,1)} %copy-done.4, bf16[1104,256]{1,0:T(8,128)(2,1)} %copy-done.3), custom_call_target="tpu_custom_call" | custom-call | tf_op jit(solution)/shard_map/exchange/pallas_call | solution.py:352
  54.4 1.0 copy-done.9
  55.4 1.1 copy-done.10
  56.5 2.9 %halo.1 = bf16[4,9,64,128]{3,2,1,0:T(8,128)(2,1)} custom-call(s32[16,8]{1,0:T(8,128)S(1)} %clamp_select_fusion.near, bf16[17,64,256]{2,1,0:T(8,128)(2,1)S(1)} %copy-done.9, bf16[17,64,256]{2,1,0:T(8,128)(2,1)S(1)} %copy-done.5, bf16[17,64,256]{2,1,0:T(8,128)(2,1)S(1)} %copy-done.10), custom_call_target="tpu_custom_call" | custom-call | tf_op jit(solution)/shard_map/halo/pallas_call | solution.py:396
  59.5 3.5 %all-to-all-start = ((bf16[4,9,64,128]{3,2,1,0:T(8,128)(2,1)}), bf16[4,9,64,128]{3,2,1,0:T(8,128)(2,1)S(1)}, u32[]{:S(2)}, u32[]{:S(2)}) async-start(bf16[4,9,64,128]{3,2,1,0:T(8,128)(2,1)} %halo.1), calls=%async_computation | async-start | bytes 1179648 | tf_op jit(solution)/shard_map/all_to_all | solution.py:410
  63.0 1.2 %copy-done.16 = bf16[4096,128]{1,0:T(8,128)(2,1)S(1)} copy-done((bf16[4096,128]{1,0:T(8,128)(2,1)S(1)}, bf16[4096,128]{1,0:T(8,128)(2,1)}, u32[]{:S(2)}) %copy-start.16) | copy-done | bytes 1048600
  64.2 8.3 %pick.2.early = bf16[8,64,512]{2,1,0:T(8,128)(2,1)S(1)} custom-call(s32[4096]{0:T(1024)S(1)} %bitcast.18, bf16[4096,128]{1,0:T(8,128)(2,1)S(1)} %copy-done.16, s32[8,1,512]{2,1,0:T(1,128)S(1)} %bitcast.17), custom_call_target="tpu_custom_call" | custom-call | flops 5000000000 | bytes 4000000 | tf_op jit(solution)/shard_map/pick/pallas_call | solution.py:409
  72.5 1.2 %copy-done.7 = bf16[4,4,64,512]{3,2,1,0:T(8,128)(2,1)S(1)} copy-done((bf16[4,4,64,512]{3,2,1,0:T(8,128)(2,1)S(1)}, bf16[4,4,64,512]{3,2,1,0:T(8,128)(2,1)}, u32[]{:S(2)}) %copy-start.7) | copy-done | bytes 1048600
  73.7 9.2 %block.1 = bf16[4,4,64,512]{3,2,1,0:T(8,128)(2,1)} custom-call(bf16[4,4,64,512]{3,2,1,0:T(8,128)(2,1)S(1)} %copy-done.7, bf16[4,9,64,128]{3,2,1,0:T(8,128)(2,1)S(1)} %all-to-all-done.rim, bf16[4,1104,256]{2,1,0:T(8,128)(2,1)S(1)} %copy-done.2), custom_call_target="tpu_custom_call" | custom-call | tf_op jit(solution)/shard_map/block/pallas_call | solution.py:412
  82.9 3.5 %all-to-all-start.1 = ((bf16[4,4,64,512]{3,2,1,0:T(8,128)(2,1)}), bf16[4,4,64,512]{3,2,1,0:T(8,128)(2,1)S(1)}, u32[]{:S(2)}, u32[]{:S(2)}) async-start(bf16[4,4,64,512]{3,2,1,0:T(8,128)(2,1)} %block.1), calls=%async_computation.1 | async-start | bytes 2097152 | tf_op jit(solution)/shard_map/all_to_all | solution.py:431
  86.6 1.2 %copy-done.17 = bf16[4096,128]{1,0:T(8,128)(2,1)S(1)} copy-done((bf16[4096,128]{1,0:T(8,128)(2,1)S(1)}, bf16[4096,128]{1,0:T(8,128)(2,1)}, u32[]{:S(2)}) %copy-start.17) | copy-done | bytes 1048600
  87.8 8.3 %pick.3.late = bf16[8,64,512]{2,1,0:T(8,128)(2,1)S(1)} custom-call(s32[4096]{0:T(1024)S(1)} %bitcast.16, bf16[4096,128]{1,0:T(8,128)(2,1)S(1)} %copy-done.17, s32[8,1,512]{2,1,0:T(1,128)S(1)} %bitcast.15), custom_call_target="tpu_custom_call" | custom-call | flops 5000000000 | bytes 4000000 | tf_op jit(solution)/shard_map/pick/pallas_call | solution.py:430
  96.1 4.8 %all-to-all-done.1 = bf16[4,4,64,512]{3,2,1,0:T(8,128)(2,1)S(1)} async-done(((bf16[4,4,64,512]{3,2,1,0:T(8,128)(2,1)}), bf16[4,4,64,512]{3,2,1,0:T(8,128)(2,1)S(1)}, u32[]{:S(2)}, u32[]{:S(2)}) %all-to-all-start.1) | async-done | bytes 1048608 | tf_op jit(solution)/shard_map/all_to_all | solution.py:431
  100.9 3.2 %finish.1 = bf16[64,16,4,128]{3,2,1,0:T(4,128)(2,1)} custom-call(bf16[16,64,512]{2,1,0:T(8,128)(2,1)S(1)} %copy-done.1, bf16[16,64,512]{2,1,0:T(8,128)(2,1)S(1)} %bitcast.11, bf16[8,64,512]{2,1,0:T(8,128)(2,1)S(1)} %pick.2.early, bf16[8,64,512]{2,1,0:T(8,128)(2,1)S(1)} %pick.3.late, s32[16,1,512]{2,1,0:T(1,128)S(1)} %bitcast.14, bf16[64,1]{1,0:T(8,128)(2,1)S(1)} %copy.16.scale), custom_call_target="tpu_custom_call" | custom-call | tf_op jit(solution)/shard_map/finish/pallas_call | solution.py:433
  (45 shorter events, 1.2 us)
Async XLA Ops:
  6.5 56.5 %all-gather.2.cloned.1.call-start = ((), (), s32[]{:S(2)}) async-start(), calls=%async_computation.2 | async-start | bytes 1310720 | tf_op jit(solution)/shard_map/all_gather | solution.py:349
  6.5 1.2 %copy-start.8 = (bf16[64,16,4,128]{3,2,1,0:T(4,128)(2,1)S(1)}, bf16[64,16,4,128]{3,2,1,0:T(4,128)(2,1)}, u32[]{:S(2)}) copy-start(bf16[64,16,4,128]{3,2,1,0:T(4,128)(2,1)} %state.1) | copy-start | bytes 3145732
  7.8 14.0 %copy-start.11 = (bf16[9,256,64]{1,2,0:T(8,128)(2,1)S(1)}, bf16[9,256,64]{1,2,0:T(8,128)(2,1)}, u32[]{:S(2)}) copy-start(bf16[9,256,64]{1,2,0:T(8,128)(2,1)} %param.16) | copy-start | bytes 884740
  7.8 14.0 %copy-start.12 = (bf16[256,256]{1,0:T(8,128)(2,1)S(1)}, bf16[256,256]{1,0:T(8,128)(2,1)}, u32[]{:S(2)}) copy-start(bf16[256,256]{1,0:T(8,128)(2,1)} %iw.1) | copy-start | bytes 393220
  7.8 14.0 %copy-start.13 = (bf16[256,256]{1,0:T(8,128)(2,1)S(1)}, bf16[256,256]{1,0:T(8,128)(2,1)}, u32[]{:S(2)}) copy-start(bf16[256,256]{1,0:T(8,128)(2,1)} %ow.1) | copy-start | bytes 393220
  7.8 15.0 %copy-start.19 = (s32[16,8]{0,1:T(8,128)S(1)}, s32[16,8]{0,1:T(8,128)}, u32[]{:S(2)}) copy-start(s32[16,8]{0,1:T(8,128)} %param.24) | copy-start | bytes 1540
  14.4 1.0 copy-start
  15.4 0.8 copy-start.4
  18.2 1.4 %copy-start.6 = (bf16[2048,384]{1,0:T(8,128)(2,1)S(1)}, bf16[2048,384]{1,0:T(8,128)(2,1)}, u32[]{:S(2)}) copy-start(bf16[2048,384]{1,0:T(8,128)(2,1)} %atm.1) | copy-start | bytes 4718596
  19.6 0.8 copy-start.14
  21.8 32.6 %copy-start.5 = (bf16[17,64,256]{2,1,0:T(8,128)(2,1)S(1)}, bf16[17,64,256]{2,1,0:T(8,128)(2,1)}, u32[]{:S(2)}) copy-start(bf16[17,64,256]{2,1,0:T(8,128)(2,1)} %copy-done.4) | copy-start | bytes 1671172
  21.9 0.8 copy-start.3
  22.8 36.6 %copy-start.18 = (s32[16,4,128]{2,1,0:T(4,128)S(1)}, s32[16,4,128]{2,1,0:T(4,128)}, u32[]{:S(2)}) copy-start(s32[16,4,128]{2,1,0:T(4,128)} %param.25) | copy-start | bytes 98308
  54.4 1.1 copy-start.9
  55.4 1.1 copy-start.10
  59.5 13.0 %all-to-all-start = ((bf16[4,9,64,128]{3,2,1,0:T(8,128)(2,1)}), bf16[4,9,64,128]{3,2,1,0:T(8,128)(2,1)S(1)}, u32[]{:S(2)}, u32[]{:S(2)}) async-start(bf16[4,9,64,128]{3,2,1,0:T(8,128)(2,1)} %halo.1), calls=%async_computation | async-start | bytes 1179648 | tf_op jit(solution)/shard_map/all_to_all | solution.py:410
  63.0 1.2 %copy-start.16 = (bf16[4096,128]{1,0:T(8,128)(2,1)S(1)}, bf16[4096,128]{1,0:T(8,128)(2,1)}, u32[]{:S(2)}) copy-start(bf16[4096,128]{1,0:T(8,128)(2,1)} %all-gather.2.cloned.1.call-done.table) | copy-start | bytes 3145732
  64.2 8.3 %copy-start.2 = (bf16[4,1104,256]{2,1,0:T(8,128)(2,1)S(1)}, bf16[4,1104,256]{2,1,0:T(8,128)(2,1)}, u32[]{:S(2)}) copy-start(bf16[4,1104,256]{2,1,0:T(8,128)(2,1)} %get-tuple-element.33.pack) | copy-start | bytes 6782980
  72.5 1.2 %copy-start.7 = (bf16[4,4,64,512]{3,2,1,0:T(8,128)(2,1)S(1)}, bf16[4,4,64,512]{3,2,1,0:T(8,128)(2,1)}, u32[]{:S(2)}) copy-start(bf16[4,4,64,512]{3,2,1,0:T(8,128)(2,1)} %get-tuple-element.31.tile) | copy-start | bytes 3145732
  73.7 12.7 %copy-start.20 = (bf16[64]{0:T(256)(128)(2,1)S(1)}, bf16[64]{0:T(256)(128)(2,1)}, u32[]{:S(2)}) copy-start(bf16[64]{0:T(256)(128)(2,1)} %param.22) | copy-start | bytes 388
  82.9 18.0 %all-to-all-start.1 = ((bf16[4,4,64,512]{3,2,1,0:T(8,128)(2,1)}), bf16[4,4,64,512]{3,2,1,0:T(8,128)(2,1)S(1)}, u32[]{:S(2)}, u32[]{:S(2)}) async-start(bf16[4,4,64,512]{3,2,1,0:T(8,128)(2,1)} %block.1), calls=%async_computation.1 | async-start | bytes 2097152 | tf_op jit(solution)/shard_map/all_to_all | solution.py:431
  86.6 1.2 %copy-start.17 = (bf16[4096,128]{1,0:T(8,128)(2,1)S(1)}, bf16[4096,128]{1,0:T(8,128)(2,1)}, u32[]{:S(2)}) copy-start(bf16[4096,128]{1,0:T(8,128)(2,1)} %all-gather.2.cloned.1.call-done.table) | copy-start | bytes 3145732
  87.8 13.1 %copy-start.1 = (bf16[16,64,512]{2,1,0:T(8,128)(2,1)S(1)}, bf16[16,64,512]{2,1,0:T(8,128)(2,1)}, u32[]{:S(2)}) copy-start(bf16[16,64,512]{2,1,0:T(8,128)(2,1)} %copy-done) | copy-start | bytes 3145732
  87.8 13.1 %copy-start.15 = (s32[16,4,128]{2,1,0:T(4,128)S(1)}, s32[16,4,128]{2,1,0:T(4,128)}, u32[]{:S(2)}) copy-start(s32[16,4,128]{2,1,0:T(4,128)} %param.23) | copy-start | bytes 98308
Sparse Core Ops, SparseCore 0:
  22.9 35.1 all-gather.1

commit v5 on v4

--- a/solution.py
+++ b/solution.py
@@ -283,14 +283,12 @@
     out[0] = total.astype(BF16)
 
 
-def finish(rows, update, early, late, mask, scale, out, scr):
+def finish(rows, update, force, mask, scale, out, scr):
     cl, some, bh, bw = out.shape
     gain = scale[:, 0:1].astype(F32)
-    first = pl.program_id(0) < pl.num_programs(0) // 2
     for j in range(some):
         total = rows[j].astype(F32) + gain * update[j].astype(F32)
-        force = jnp.where(first, early[j].astype(F32), late[j].astype(F32))
-        total = (total + force) * mask[j].astype(F32)
+        total = (total + force[j].astype(F32)) * mask[j].astype(F32)
         for i in range(bh):
             scr[:, i, :] = total[:, i * bw : (i + 1) * bw]
         out[:, j] = scr[...].astype(BF16)
@@ -346,13 +344,12 @@
         name="flux_rows",
     )(atmos, flux_weight.T)
     rows, strips, pack_local, table = lax.optimization_barrier((rows, strips, pack_local, table))
-    table = lax.all_gather(table, "tile", axis=0, tiled=True)
-
-    anywhere = pl.BlockSpec(memory_space=pl.ANY)
+
+    resident = pl.BlockSpec(memory_space=pltpu.VMEM)
     tile, below, above, pack = pl.pallas_call(
         exchange,
-        in_specs=[anywhere] * 3,
-        out_specs=[anywhere] * 4,
+        in_specs=[resident] * 3,
+        out_specs=[resident] * 4,
         out_shape=[
             jax.ShapeDtypeStruct((groups, per, cl, cells), BF16),
             jax.ShapeDtypeStruct(strips.shape, BF16),
@@ -366,9 +363,13 @@
             pltpu.SemaphoreType.DMA((groups,)),
             pltpu.SemaphoreType.DMA((2,)),
         ],
-        compiler_params=pltpu.CompilerParams(collective_id=0, has_side_effects=True),
+        compiler_params=pltpu.CompilerParams(
+            collective_id=0, has_side_effects=True, vmem_limit_bytes=LIMIT
+        ),
         name="exchange",
     )(rows.reshape(groups, per, cl, cells), strips, pack_local)
+    below, above, table = lax.optimization_barrier((below, above, table))
+    table = lax.all_gather(table, "tile", axis=0, tiled=True)
     local = lax.rem(remap, trows * parts)
     flat = (remap // (trows * parts)) * trows + lax.rem(local, trows)
     which = (local // trows).reshape(slots, 1, cells)
@@ -377,17 +378,17 @@
         functools.partial(pick, cl=cl),
         grid_spec=pltpu.PrefetchScalarGridSpec(
             num_scalar_prefetch=1,
-            grid=(slots // 2,),
+            grid=(slots,),
             in_specs=[whole(tiles * trows, 128), lane_spec],
             out_specs=slot_spec,
             scratch_shapes=[pltpu.VMEM((tiles * trows, 128), F32), pltpu.VMEM((cells, 128), F32)],
         ),
-        out_shape=jax.ShapeDtypeStruct((slots // 2, cl, cells), BF16),
-        compiler_params=params(),
-        cost_estimate=pl.CostEstimate(flops=5 * 10**9, bytes_accessed=4 * 10**6, transcendentals=0),
+        out_shape=jax.ShapeDtypeStruct((slots, cl, cells), BF16),
+        compiler_params=params(),
+        cost_estimate=pl.CostEstimate(flops=10**10, bytes_accessed=4 * 10**6, transcendentals=0),
         name="pick",
     )
-    flat, half = flat.reshape(2, -1), slots // 2
+    flat = flat.reshape(-1)
 
     first = (lax.axis_index("tile") - 1) * slots
     near = jnp.where(neighbours >= 0, jnp.clip(neighbours - first, 0, 3 * slots - 1), -1)
@@ -405,10 +406,7 @@
         compiler_params=params(),
         name="halo",
     )(near, below, strips, above)
-    early, rim = lax.optimization_barrier((flat[0], rim))
-    early = picks(early, table, which[:half])
     rim = lax.all_to_all(rim, ("chan", "sec"), split_axis=0, concat_axis=0)
-    early, tile = lax.optimization_barrier((early, tile))
     update = pl.pallas_call(
         functools.partial(block, hl=hl),
         grid=(per,),
@@ -426,17 +424,14 @@
         compiler_params=params(),
         name="block",
     )(tile, rim, pack)
-    late, update = lax.optimization_barrier((flat[1], update))
-    late = picks(late, table, which[half:])
+    flat, update = lax.optimization_barrier((flat, update))
+    forcing = picks(flat, table, which)
     update = lax.all_to_all(update, ("chan", "sec"), split_axis=0, concat_axis=0)
-    last = half // some - 1
     return pl.pallas_call(
         finish,
         grid=(slots // some,),
         in_specs=[
-            some_spec, some_spec,
-            pl.BlockSpec((some, cl, cells), lambda s: (jnp.minimum(s, last), 0, 0)),
-            pl.BlockSpec((some, cl, cells), lambda s: (jnp.maximum(s - last - 1, 0), 0, 0)),
+            some_spec, some_spec, some_spec,
             pl.BlockSpec((some, 1, cells), lambda s: (s, 0, 0)), whole(cl, 1),
         ],
         out_specs=state_spec,
@@ -447,8 +442,7 @@
     )(
         rows,
         update.reshape(slots, cl, cells),
-        early,
-        late,
+        forcing,
         cell_mask.reshape(slots, 1, cells),
         layer_scale.reshape(cl, 1),
     )

time: 112 us -> 110 us (0.982)
  waiting for transfers between devices: 4.85 us -> 9.47 us
  local copies, waits for them, and re-layouts: 14 us -> 10.3 us
  Pallas kernels: 71.3 us -> 69.2 us
    all_to_all x1, waiting for transfers between devices: 0.01 us -> 9.43 us  [on_device(): rim = lax.all_to_all(rim, ('chan', 'sec'), split_axis=0, concat_axis=0)]
    all_to_all x1, waiting for transfers between devices: 4.81 us -> 0.01 us  [on_device(): lax.all_to_all(update, ('chan', 'sec'), split_axis=0, concat_axis=0)]
    unnamed x43 -> x29, local copies, waits for them, and re-layouts: 11.9 us -> 8.24 us
    pallas_call x3 -> x2, Pallas kernels: 48 us -> 45.9 us  [the longest x1 30 us: on_device(): pl.pallas_call(exchange, in_specs=[resident] * 3, out_specs=[resident] *...]
  transfers between devices with their start and end apart: 3 -> 3, of which waited for: 1 -> 1; matrix products, arithmetic and copies ran while one was open for 0% -> 0% of each run, Pallas kernels for 46% -> 25%
where the time goes in v5:
time: 110 us
  Pallas kernels  69.2 us (63%)
  between operations  13.5 us (12%)
  local copies, waits for them, and re-layouts  10.3 us (9%)
  waiting for transfers between devices  9.47 us (9%)
  starting transfers between devices  7 us (6%)
    pallas_call x1, Pallas kernels, on_device(): pl.pallas_call(exchange, in_specs=[resident] * 3, out_specs=[resident] *...  30 us
    pallas_call x1, Pallas kernels, on_device(): forcing = picks(flat, table, which)  15.8 us
    all_to_all x1, waiting for transfers between devices, on_device(): rim = lax.all_to_all(rim, ('chan', 'sec'), split_axis=0, concat_axis=0)  9.43 us
    pallas_call x1, Pallas kernels, on_device(): pl.pallas_call(functools.partial(block, hl=hl), grid=(per,), in_specs=[pl...  9.2 us
    unnamed x29, local copies, waits for them, and re-layouts  8.24 us
    pallas_call x1, Pallas kernels, on_device(): pl.pallas_call(split_rows, grid=(slots // some,), in_specs=[state_spec],...  6.61 us
    all_to_all x1, starting transfers between devices, on_device(): lax.all_to_all(update, ('chan', 'sec'), split_axis=0, concat_axis=0)  3.52 us
    all_to_all x1, starting transfers between devices, on_device(): rim = lax.all_to_all(rim, ('chan', 'sec'), split_axis=0, concat_axis=0)  3.48 us
  transfers between devices with their start and end apart: 3, of which 1 were waited for; matrix products, arithmetic and copies ran while one was open for 0% of the time, Pallas kernels for 25%

profile of v5, /device:TPU:0, one launch (start us, length us, event | category | flops | bytes accessed | tf_op | source)
XLA Modules:
  0.0 109.7 jit_solution(17692547472500343016)
XLA Ops:
  6.5 1.2 %copy-done.2 = bf16[64,16,4,128]{3,2,1,0:T(4,128)(2,1)S(1)} copy-done((bf16[64,16,4,128]{3,2,1,0:T(4,128)(2,1)S(1)}, bf16[64,16,4,128]{3,2,1,0:T(4,128)(2,1)}, u32[]{:S(2)}) %copy-start.2) | copy-done | bytes 1048600
  7.8 6.6 %split_rows.1 = (bf16[16,64,512]{2,1,0:T(8,128)(2,1)S(1)}, bf16[17,64,256]{2,1,0:T(8,128)(2,1)S(1)}) custom-call(bf16[64,16,4,128]{3,2,1,0:T(4,128)(2,1)S(1)} %copy-done.2), custom_call_target="tpu_custom_call" | custom-call | tf_op jit(solution)/shard_map/split_rows/pallas_call | solution.py:313
  14.4 0.7 pad.11
  15.1 0.7 pad.12
  15.7 0.7 stack.12
  16.4 1.4 %copy-done.1 = bf16[2048,384]{1,0:T(8,128)(2,1)S(1)} copy-done((bf16[2048,384]{1,0:T(8,128)(2,1)S(1)}, bf16[2048,384]{1,0:T(8,128)(2,1)}, u32[]{:S(2)}) %copy-start.1) | copy-done | bytes 1572888
  17.8 0.8 copy-done.8
  18.6 1.3 %flux_rows.1 = bf16[1024,128]{1,0:T(8,128)(2,1)} custom-call(bf16[2048,384]{1,0:T(8,128)(2,1)S(1)} %copy-done.1, bf16[64,384]{1,0:T(8,128)(2,1)S(1)} %bitcast.11), custom_call_target="tpu_custom_call" | custom-call | tf_op jit(solution)/shard_map/flux_rows/pallas_call | solution.py:340
  19.9 0.1 pack_weights.1.pack
  20.1 30.0 %exchange.1 = (bf16[4,4,64,512]{3,2,1,0:T(8,128)(2,1)S(1)}, bf16[17,64,256]{2,1,0:T(8,128)(2,1)S(1)}, bf16[17,64,256]{2,1,0:T(8,128)(2,1)S(1)}, bf16[4,1104,256]{2,1,0:T(8,128)(2,1)}) custom-call(bf16[4,4,64,512]{3,2,1,0:T(8,128)(2,1)S(1)} %bitcast.8, bf16[17,64,256]{2,1,0:T(8,128)(2,1)S(1)} %get-tuple-element.23.strips.mine, ...), custom_call_target="tpu_custom_call" | custom-call | tf_op jit(solution)/shard_map/exchange/pallas_call | solution.py:349
  50.1 0.8 copy-done.3
  51.0 0.1 copy.14
  51.0 1.1 copy-done.4
  52.1 2.9 %halo.1 = bf16[4,9,64,128]{3,2,1,0:T(8,128)(2,1)} custom-call(s32[16,8]{1,0:T(8,128)S(1)} %clamp_select_fusion.near, bf16[17,64,256]{2,1,0:T(8,128)(2,1)S(1)} %get-tuple-element.29.below, bf16[17,64,256]{2,1,0:T(8,128)(2,1)S(1)} %get-tuple-element.23.strips.mine, bf16[17,64,256]{2,1,0:T(8,128)(2,1)S(1)} %copy-done.4), custom_call_target="tpu_custom_call" | custom-call | tf_op jit(solution)/shard_map/halo/pallas_call | solution.py:397
  55.0 3.5 %all-to-all-start = ((bf16[4,9,64,128]{3,2,1,0:T(8,128)(2,1)}), bf16[4,9,64,128]{3,2,1,0:T(8,128)(2,1)S(1)}, u32[]{:S(2)}, u32[]{:S(2)}) async-start(bf16[4,9,64,128]{3,2,1,0:T(8,128)(2,1)} %halo.1), calls=%async_computation | async-start | bytes 1179648 | tf_op jit(solution)/shard_map/all_to_all | solution.py:409
  58.5 0.1 copy.16.scale
  58.6 0.1 add_select_fusion
  58.7 9.4 %all-to-all-done.rim = bf16[4,9,64,128]{3,2,1,0:T(8,128)(2,1)S(1)} async-done(((bf16[4,9,64,128]{3,2,1,0:T(8,128)(2,1)}), bf16[4,9,64,128]{3,2,1,0:T(8,128)(2,1)S(1)}, u32[]{:S(2)}, u32[]{:S(2)}) %all-to-all-start) | async-done | bytes 589856 | tf_op jit(solution)/shard_map/all_to_all | solution.py:409
  68.2 1.6 %copy-done = bf16[4,1104,256]{2,1,0:T(8,128)(2,1)S(1)} copy-done((bf16[4,1104,256]{2,1,0:T(8,128)(2,1)S(1)}, bf16[4,1104,256]{2,1,0:T(8,128)(2,1)}, u32[]{:S(2)}) %copy-start) | copy-done | bytes 2261016
  69.8 9.2 %block.1 = bf16[4,4,64,512]{3,2,1,0:T(8,128)(2,1)} custom-call(bf16[4,4,64,512]{3,2,1,0:T(8,128)(2,1)S(1)} %get-tuple-element.25.tile, bf16[4,9,64,128]{3,2,1,0:T(8,128)(2,1)S(1)} %all-to-all-done.rim, bf16[4,1104,256]{2,1,0:T(8,128)(2,1)S(1)} %copy-done), custom_call_target="tpu_custom_call" | custom-call | tf_op jit(solution)/shard_map/block/pallas_call | solution.py:410
  79.0 3.5 %all-to-all-start.1 = ((bf16[4,4,64,512]{3,2,1,0:T(8,128)(2,1)}), bf16[4,4,64,512]{3,2,1,0:T(8,128)(2,1)S(1)}, u32[]{:S(2)}, u32[]{:S(2)}) async-start(bf16[4,4,64,512]{3,2,1,0:T(8,128)(2,1)} %block.1), calls=%async_computation.1 | async-start | bytes 2097152 | tf_op jit(solution)/shard_map/all_to_all | solution.py:429
  82.6 1.2 %copy-done.10 = bf16[4096,128]{1,0:T(8,128)(2,1)S(1)} copy-done((bf16[4096,128]{1,0:T(8,128)(2,1)S(1)}, bf16[4096,128]{1,0:T(8,128)(2,1)}, u32[]{:S(2)}) %copy-start.10) | copy-done | bytes 1048600
  83.8 15.8 %pick.1.force = bf16[16,64,512]{2,1,0:T(8,128)(2,1)S(1)} custom-call(s32[8192]{0:T(1024)S(1)} %bitcast.14, bf16[4096,128]{1,0:T(8,128)(2,1)S(1)} %copy-done.10, s32[16,1,512]{2,1,0:T(1,128)S(1)} %bitcast.13), custom_call_target="tpu_custom_call" | custom-call | flops 10000000000 | bytes 4000000 | tf_op jit(solution)/shard_map/pick/pallas_call | solution.py:428
  99.6 3.2 %finish.1 = bf16[64,16,4,128]{3,2,1,0:T(4,128)(2,1)} custom-call(bf16[16,64,512]{2,1,0:T(8,128)(2,1)S(1)} %get-tuple-element.22.rows, bf16[16,64,512]{2,1,0:T(8,128)(2,1)S(1)} %bitcast.9, bf16[16,64,512]{2,1,0:T(8,128)(2,1)S(1)} %pick.1.force, s32[16,1,512]{2,1,0:T(1,128)S(1)} %bitcast.12, bf16[64,1]{1,0:T(8,128)(2,1)S(1)} %copy.16.scale), custom_call_target="tpu_custom_call" | custom-call | tf_op jit(solution)/shard_map/finish/pallas_call | solution.py:430
  (29 shorter events, 0.1 us)
Async XLA Ops:
  6.5 76.0 %all-gather.2.cloned.1.call-start = ((), (), s32[]{:S(2)}) async-start(), calls=%async_computation.2 | async-start | bytes 1310720 | tf_op jit(solution)/shard_map/all_gather | solution.py:372
  6.5 1.2 %copy-start.2 = (bf16[64,16,4,128]{3,2,1,0:T(4,128)(2,1)S(1)}, bf16[64,16,4,128]{3,2,1,0:T(4,128)(2,1)}, u32[]{:S(2)}) copy-start(bf16[64,16,4,128]{3,2,1,0:T(4,128)(2,1)} %state.1) | copy-start | bytes 3145732
  7.8 12.2 %copy-start.5 = (bf16[9,256,64]{1,2,0:T(8,128)(2,1)S(1)}, bf16[9,256,64]{1,2,0:T(8,128)(2,1)}, u32[]{:S(2)}) copy-start(bf16[9,256,64]{1,2,0:T(8,128)(2,1)} %param.16) | copy-start | bytes 884740
  7.8 12.2 %copy-start.6 = (bf16[256,256]{1,0:T(8,128)(2,1)S(1)}, bf16[256,256]{1,0:T(8,128)(2,1)}, u32[]{:S(2)}) copy-start(bf16[256,256]{1,0:T(8,128)(2,1)} %iw.1) | copy-start | bytes 393220
  7.8 12.2 %copy-start.7 = (bf16[256,256]{1,0:T(8,128)(2,1)S(1)}, bf16[256,256]{1,0:T(8,128)(2,1)}, u32[]{:S(2)}) copy-start(bf16[256,256]{1,0:T(8,128)(2,1)} %ow.1) | copy-start | bytes 393220
  16.4 1.4 %copy-start.1 = (bf16[2048,384]{1,0:T(8,128)(2,1)S(1)}, bf16[2048,384]{1,0:T(8,128)(2,1)}, u32[]{:S(2)}) copy-start(bf16[2048,384]{1,0:T(8,128)(2,1)} %atm.1) | copy-start | bytes 4718596
  17.8 0.8 copy-start.8
  19.9 31.0 %copy-start.12 = (s32[16,8]{0,1:T(8,128)S(1)}, s32[16,8]{0,1:T(8,128)}, u32[]{:S(2)}) copy-start(s32[16,8]{0,1:T(8,128)} %param.24) | copy-start | bytes 1540
  50.1 0.8 copy-start.3
  50.9 7.6 %copy-start.13 = (bf16[64]{0:T(256)(128)(2,1)S(1)}, bf16[64]{0:T(256)(128)(2,1)}, u32[]{:S(2)}) copy-start(bf16[64]{0:T(256)(128)(2,1)} %param.22) | copy-start | bytes 388
  50.9 7.7 %copy-start.11 = (s32[16,4,128]{2,1,0:T(4,128)S(1)}, s32[16,4,128]{2,1,0:T(4,128)}, u32[]{:S(2)}) copy-start(s32[16,4,128]{2,1,0:T(4,128)} %param.25) | copy-start | bytes 98308
  51.0 1.1 copy-start.4
  55.0 13.1 %all-to-all-start = ((bf16[4,9,64,128]{3,2,1,0:T(8,128)(2,1)}), bf16[4,9,64,128]{3,2,1,0:T(8,128)(2,1)S(1)}, u32[]{:S(2)}, u32[]{:S(2)}) async-start(bf16[4,9,64,128]{3,2,1,0:T(8,128)(2,1)} %halo.1), calls=%async_computation | async-start | bytes 1179648 | tf_op jit(solution)/shard_map/all_to_all | solution.py:409
  68.2 1.6 %copy-start = (bf16[4,1104,256]{2,1,0:T(8,128)(2,1)S(1)}, bf16[4,1104,256]{2,1,0:T(8,128)(2,1)}, u32[]{:S(2)}) copy-start(bf16[4,1104,256]{2,1,0:T(8,128)(2,1)} %get-tuple-element.31.pack) | copy-start | bytes 6782980
  79.0 20.6 %all-to-all-start.1 = ((bf16[4,4,64,512]{3,2,1,0:T(8,128)(2,1)}), bf16[4,4,64,512]{3,2,1,0:T(8,128)(2,1)S(1)}, u32[]{:S(2)}, u32[]{:S(2)}) async-start(bf16[4,4,64,512]{3,2,1,0:T(8,128)(2,1)} %block.1), calls=%async_computation.1 | async-start | bytes 2097152 | tf_op jit(solution)/shard_map/all_to_all | solution.py:429
  82.6 1.2 %copy-start.10 = (bf16[4096,128]{1,0:T(8,128)(2,1)S(1)}, bf16[4096,128]{1,0:T(8,128)(2,1)}, u32[]{:S(2)}) copy-start(bf16[4096,128]{1,0:T(8,128)(2,1)} %all-gather.2.cloned.1.call-done.table) | copy-start | bytes 3145732
  83.8 15.8 %copy-start.9 = (s32[16,4,128]{2,1,0:T(4,128)S(1)}, s32[16,4,128]{2,1,0:T(4,128)}, u32[]{:S(2)}) copy-start(s32[16,4,128]{2,1,0:T(4,128)} %param.23) | copy-start | bytes 98308
Sparse Core Ops, SparseCore 0:
  51.1 28.0 all-gather.1

commit v6 on v3

--- a/solution.py
+++ b/solution.py
@@ -306,11 +306,11 @@
     pack = lax.all_gather(pack_local, ("chan", "sec"), axis=0)
 
     rows, strips, _ = lax.optimization_barrier((rows, strips, pack_local))
-    anywhere = pl.BlockSpec(memory_space=pl.ANY)
+    resident = pl.BlockSpec(memory_space=pltpu.VMEM)
     tile, below, above = pl.pallas_call(
         exchange,
-        in_specs=[anywhere, anywhere],
-        out_specs=[anywhere] * 3,
+        in_specs=[resident, resident],
+        out_specs=[resident] * 3,
         out_shape=[
             jax.ShapeDtypeStruct((groups, per, cl, cells), BF16),
             jax.ShapeDtypeStruct(strips.shape, BF16),
@@ -321,7 +321,9 @@
             pltpu.SemaphoreType.DMA((groups + 2,)),
             pltpu.SemaphoreType.DMA,
         ],
-        compiler_params=pltpu.CompilerParams(collective_id=0, has_side_effects=True),
+        compiler_params=pltpu.CompilerParams(
+            collective_id=0, has_side_effects=True, vmem_limit_bytes=LIMIT
+        ),
         name="exchange",
     )(rows.reshape(groups, per, cl, cells), strips)
     below, above, atmos = lax.optimization_barrier((below, above, atmos))

time: 107 us -> 111 us (1.037)
  local copies, waits for them, and re-layouts: 9.78 us -> 13.9 us
    unnamed x39 -> x37, local copies, waits for them, and re-layouts: 7.53 us -> 11.7 us
  transfers between devices with their start and end apart: 4 -> 4, of which waited for: 2 -> 1; matrix products, arithmetic and copies ran while one was open for 0% -> 0% of each run, Pallas kernels for 58% -> 56%
where the time goes in v6:
time: 111 us; the launch traced here: 110 us
  Pallas kernels  66.1 us (60%)
  local copies, waits for them, and re-layouts  13.9 us (13%)
  between operations  13.5 us (12%)
  waiting for transfers between devices  9.48 us (9%)
  starting transfers between devices  7.04 us (6%)
    pallas_call x1, Pallas kernels, on_device(): pl.pallas_call(exchange, in_specs=[resident, resident], out_specs=[reside...  26.1 us
    pallas_call x1, Pallas kernels, on_device(): pl.pallas_call(functools.partial(pick, cl=cl), grid_spec=pltpu.PrefetchSc...  15.8 us
    unnamed x37, local copies, waits for them, and re-layouts  11.7 us
    all_to_all x1, waiting for transfers between devices, on_device(): rim = lax.all_to_all(rim, ('chan', 'sec'), split_axis=0, concat_axis=0)  9.42 us
    pallas_call x1, Pallas kernels, on_device(): pl.pallas_call(functools.partial(block, hl=hl), grid=(per,), in_specs=[pl...  9.2 us
    pallas_call x1, Pallas kernels, on_device(): pl.pallas_call(split_rows, grid=(slots // some,), in_specs=[state_spec],...  6.61 us
    all_to_all x1, starting transfers between devices, on_device(): lax.all_to_all(update, ('chan', 'sec'), split_axis=0, concat_axis=0)  3.52 us
    all_to_all x1, starting transfers between devices, on_device(): rim = lax.all_to_all(rim, ('chan', 'sec'), split_axis=0, concat_axis=0)  3.48 us
  transfers between devices with their start and end apart: 4, of which 1 were waited for; matrix products, arithmetic and copies ran while one was open for 0% of the time, Pallas kernels for 56%

profile of v6, /device:TPU:0, one launch (start us, length us, event | category | flops | bytes accessed | tf_op | source)
XLA Modules:
  0.0 110.2 jit_solution(16684304511916213608)
XLA Ops:
  6.5 0.8 pad.11
  7.3 0.7 pad.12
  8.7 1.0 copy-done.9
  9.6 0.9 copy-done.10
  10.5 0.9 copy-done.11
  11.4 0.9 pack_weights.1
  12.5 1.2 %copy-done.4 = bf16[64,16,4,128]{3,2,1,0:T(4,128)(2,1)S(1)} copy-done((bf16[64,16,4,128]{3,2,1,0:T(4,128)(2,1)S(1)}, bf16[64,16,4,128]{3,2,1,0:T(4,128)(2,1)}, u32[]{:S(2)}) %copy-start.4) | copy-done | bytes 1048600
  13.7 6.6 %split_rows.1 = (bf16[16,64,512]{2,1,0:T(8,128)(2,1)S(1)}, bf16[17,64,256]{2,1,0:T(8,128)(2,1)S(1)}) custom-call(bf16[64,16,4,128]{3,2,1,0:T(4,128)(2,1)S(1)} %copy-done.4), custom_call_target="tpu_custom_call" | custom-call | tf_op jit(solution)/shard_map/split_rows/pallas_call | solution.py:282
  20.3 26.1 %exchange.1 = (bf16[4,4,64,512]{3,2,1,0:T(8,128)(2,1)S(1)}, bf16[17,64,256]{2,1,0:T(8,128)(2,1)S(1)}, bf16[17,64,256]{2,1,0:T(8,128)(2,1)S(1)}) custom-call(bf16[4,4,64,512]{3,2,1,0:T(8,128)(2,1)S(1)} %bitcast.9, bf16[17,64,256]{2,1,0:T(8,128)(2,1)S(1)} %get-tuple-element.18.strips.mine), custom_call_target="tpu_custom_call" | custom-call | tf_op jit(solution)/shard_map/exchange/pallas_call | solution.py:310
  46.4 1.0 copy-done.2
  47.4 0.8 copy-done.5
  48.2 0.8 copy-done.7
  49.1 1.3 %flux_rows.1 = bf16[1024,128]{1,0:T(8,128)(2,1)} custom-call(bf16[2048,384]{1,0:T(8,128)(2,1)S(1)} %copy-done.1, bf16[64,384]{1,0:T(8,128)(2,1)S(1)} %bitcast.13), custom_call_target="tpu_custom_call" | custom-call | tf_op jit(solution)/shard_map/flux_rows/pallas_call | solution.py:332
  50.5 1.1 %copy-done.6 = bf16[17,64,256]{2,1,0:T(8,128)(2,1)S(1)} copy-done((bf16[17,64,256]{2,1,0:T(8,128)(2,1)S(1)}, bf16[17,64,256]{2,1,0:T(8,128)(2,1)}, u32[]{:S(2)}) %copy-start.6) | copy-done | bytes 557080
  51.6 1.1 copy-done.8
  52.7 2.9 %halo.1 = bf16[4,9,64,128]{3,2,1,0:T(8,128)(2,1)} custom-call(s32[16,8]{1,0:T(8,128)S(1)} %clamp_select_fusion.near, bf16[17,64,256]{2,1,0:T(8,128)(2,1)S(1)} %copy-done.6, bf16[17,64,256]{2,1,0:T(8,128)(2,1)S(1)} %get-tuple-element.18.strips.mine, bf16[17,64,256]{2,1,0:T(8,128)(2,1)S(1)} %copy-done.8), custom_call_target="tpu_custom_call" | custom-call | tf_op jit(solution)/shard_map/halo/pallas_call | solution.py:363
  55.6 3.5 %all-to-all-start = ((bf16[4,9,64,128]{3,2,1,0:T(8,128)(2,1)}), bf16[4,9,64,128]{3,2,1,0:T(8,128)(2,1)S(1)}, u32[]{:S(2)}, u32[]{:S(2)}) async-start(bf16[4,9,64,128]{3,2,1,0:T(8,128)(2,1)} %halo.1), calls=%async_computation | async-start | bytes 1179648 | tf_op jit(solution)/shard_map/all_to_all | solution.py:375
  59.3 9.4 %all-to-all-done.rim = bf16[4,9,64,128]{3,2,1,0:T(8,128)(2,1)S(1)} async-done(((bf16[4,9,64,128]{3,2,1,0:T(8,128)(2,1)}), bf16[4,9,64,128]{3,2,1,0:T(8,128)(2,1)S(1)}, u32[]{:S(2)}, u32[]{:S(2)}) %all-to-all-start) | async-done | bytes 589856 | tf_op jit(solution)/shard_map/all_to_all | solution.py:375
  68.7 1.7 %copy-done = bf16[4416,256]{1,0:T(8,128)(2,1)S(1)} copy-done((bf16[4416,256]{1,0:T(8,128)(2,1)S(1)}, bf16[4416,256]{1,0:T(8,128)(2,1)}, u32[]{:S(2)}) %copy-start) | copy-done | bytes 2261016
  70.4 9.2 %block.1 = bf16[4,4,64,512]{3,2,1,0:T(8,128)(2,1)} custom-call(bf16[4,4,64,512]{3,2,1,0:T(8,128)(2,1)S(1)} %copy-done.3, bf16[4,9,64,128]{3,2,1,0:T(8,128)(2,1)S(1)} %all-to-all-done.rim, bf16[4,1104,256]{2,1,0:T(8,128)(2,1)S(1)} %bitcast.11), custom_call_target="tpu_custom_call" | custom-call | tf_op jit(solution)/shard_map/block/pallas_call | solution.py:376
  79.6 3.5 %all-to-all-start.1 = ((bf16[4,4,64,512]{3,2,1,0:T(8,128)(2,1)}), bf16[4,4,64,512]{3,2,1,0:T(8,128)(2,1)S(1)}, u32[]{:S(2)}, u32[]{:S(2)}) async-start(bf16[4,4,64,512]{3,2,1,0:T(8,128)(2,1)} %block.1), calls=%async_computation.1 | async-start | bytes 2097152 | tf_op jit(solution)/shard_map/all_to_all | solution.py:393
  83.2 1.2 %copy-done.14 = bf16[4096,128]{1,0:T(8,128)(2,1)S(1)} copy-done((bf16[4096,128]{1,0:T(8,128)(2,1)S(1)}, bf16[4096,128]{1,0:T(8,128)(2,1)}, u32[]{:S(2)}) %copy-start.14) | copy-done | bytes 1048600
  84.4 15.8 %pick.1.force = bf16[16,64,512]{2,1,0:T(8,128)(2,1)S(1)} custom-call(s32[8192]{0:T(1024)S(1)} %bitcast.16, bf16[4096,128]{1,0:T(8,128)(2,1)S(1)} %copy-done.14, s32[16,1,512]{2,1,0:T(1,128)S(1)} %bitcast.15), custom_call_target="tpu_custom_call" | custom-call | flops 10000000000 | bytes 4000000 | tf_op jit(solution)/shard_map/pick/pallas_call | solution.py:344
  100.2 3.2 %finish.1 = bf16[64,16,4,128]{3,2,1,0:T(4,128)(2,1)} custom-call(bf16[16,64,512]{2,1,0:T(8,128)(2,1)S(1)} %get-tuple-element.17.rows, bf16[16,64,512]{2,1,0:T(8,128)(2,1)S(1)} %bitcast.10, bf16[16,64,512]{2,1,0:T(8,128)(2,1)S(1)} %pick.1.force, s32[16,1,512]{2,1,0:T(1,128)S(1)} %bitcast.14, bf16[64,1]{1,0:T(8,128)(2,1)S(1)} %copy.16.scale), custom_call_target="tpu_custom_call" | custom-call | tf_op jit(solution)/shard_map/finish/pallas_call | solution.py:394
  (40 shorter events, 1.1 us)
Async XLA Ops:
  6.5 42.5 %copy-start.1 = (bf16[2048,384]{1,0:T(8,128)(2,1)S(1)}, bf16[2048,384]{1,0:T(8,128)(2,1)}, u32[]{:S(2)}) copy-start(bf16[2048,384]{1,0:T(8,128)(2,1)} %atm) | copy-start | bytes 4718596
  6.5 62.2 %all-gather.6.cloned.1.call-start = ((), (), s32[]{:S(2)}) async-start(), calls=%async_computation.3 | async-start | bytes 2826240 | tf_op jit(solution)/shard_map/all_gather | solution.py:306
  8.7 1.0 copy-start.9
  9.6 0.9 copy-start.10
  10.5 0.9 copy-start.11
  11.4 37.6 %copy-start.12 = (bf16[384,64]{0,1:T(8,128)(2,1)S(1)}, bf16[384,64]{0,1:T(8,128)(2,1)}, u32[]{:S(2)}) copy-start(bf16[384,64]{0,1:T(8,128)(2,1)} %param.15) | copy-start | bytes 147460
  12.4 70.8 %all-gather.4.cloned.1.call-start = ((), (), s32[]{:S(2)}) async-start(), calls=%async_computation.2 | async-start | bytes 1310720 | tf_op jit(solution)/shard_map/all_gather | solution.py:338
  12.4 1.2 %copy-start.4 = (bf16[64,16,4,128]{3,2,1,0:T(4,128)(2,1)S(1)}, bf16[64,16,4,128]{3,2,1,0:T(4,128)(2,1)}, u32[]{:S(2)}) copy-start(bf16[64,16,4,128]{3,2,1,0:T(4,128)(2,1)} %state.1) | copy-start | bytes 3145732
  13.7 36.8 %copy-start.16 = (s32[16,8]{0,1:T(8,128)S(1)}, s32[16,8]{0,1:T(8,128)}, u32[]{:S(2)}) copy-start(s32[16,8]{0,1:T(8,128)} %param.24) | copy-start | bytes 1540
  46.4 1.0 copy-start.2
  47.4 0.8 copy-start.5
  48.2 0.8 copy-start.7
  49.0 10.1 %copy-start.17 = (bf16[64]{0:T(256)(128)(2,1)S(1)}, bf16[64]{0:T(256)(128)(2,1)}, u32[]{:S(2)}) copy-start(bf16[64]{0:T(256)(128)(2,1)} %param.22) | copy-start | bytes 388
  49.0 10.2 %copy-start.15 = (s32[16,4,128]{2,1,0:T(4,128)S(1)}, s32[16,4,128]{2,1,0:T(4,128)}, u32[]{:S(2)}) copy-start(s32[16,4,128]{2,1,0:T(4,128)} %param.25) | copy-start | bytes 98308
  50.4 18.4 %copy-start.3 = (bf16[4,4,64,512]{3,2,1,0:T(8,128)(2,1)S(1)}, bf16[4,4,64,512]{3,2,1,0:T(8,128)(2,1)}, u32[]{:S(2)}) copy-start(bf16[4,4,64,512]{3,2,1,0:T(8,128)(2,1)} %copy-done.2) | copy-start | bytes 3145732
  50.5 1.1 %copy-start.6 = (bf16[17,64,256]{2,1,0:T(8,128)(2,1)S(1)}, bf16[17,64,256]{2,1,0:T(8,128)(2,1)}, u32[]{:S(2)}) copy-start(bf16[17,64,256]{2,1,0:T(8,128)(2,1)} %copy-done.5) | copy-start | bytes 1671172
  51.6 1.1 copy-start.8
  55.6 13.1 %all-to-all-start = ((bf16[4,9,64,128]{3,2,1,0:T(8,128)(2,1)}), bf16[4,9,64,128]{3,2,1,0:T(8,128)(2,1)S(1)}, u32[]{:S(2)}, u32[]{:S(2)}) async-start(bf16[4,9,64,128]{3,2,1,0:T(8,128)(2,1)} %halo.1), calls=%async_computation | async-start | bytes 1179648 | tf_op jit(solution)/shard_map/all_to_all | solution.py:375
  68.7 1.7 %copy-start = (bf16[4416,256]{1,0:T(8,128)(2,1)S(1)}, bf16[4416,256]{1,0:T(8,128)(2,1)}, u32[]{:S(2)}) copy-start(bf16[4416,256]{1,0:T(8,128)(2,1)} %all-gather.6.cloned.1.call-done) | copy-start | bytes 6782980
  79.6 20.6 %all-to-all-start.1 = ((bf16[4,4,64,512]{3,2,1,0:T(8,128)(2,1)}), bf16[4,4,64,512]{3,2,1,0:T(8,128)(2,1)S(1)}, u32[]{:S(2)}, u32[]{:S(2)}) async-start(bf16[4,4,64,512]{3,2,1,0:T(8,128)(2,1)} %block.1), calls=%async_computation.1 | async-start | bytes 2097152 | tf_op jit(solution)/shard_map/all_to_all | solution.py:393
  83.1 1.2 %copy-start.14 = (bf16[4096,128]{1,0:T(8,128)(2,1)S(1)}, bf16[4096,128]{1,0:T(8,128)(2,1)}, u32[]{:S(2)}) copy-start(bf16[4096,128]{1,0:T(8,128)(2,1)} %all-gather.4.cloned.1.call-done.table) | copy-start | bytes 3145732
  84.4 15.8 %copy-start.13 = (s32[16,4,128]{2,1,0:T(4,128)S(1)}, s32[16,4,128]{2,1,0:T(4,128)}, u32[]{:S(2)}) copy-start(s32[16,4,128]{2,1,0:T(4,128)} %param.23) | copy-start | bytes 98308
Sparse Core Ops, SparseCore 0:
  12.5 35.9 all-gather.5
  50.5 29.9 all-gather.3
